TPU v7x, 256 devices: a whole 4x4x8 slice. The times are simulated.
256 devices in a mesh: gx: 16 (over x, y_lo, core), gz: 16 (over y_hi, z).
Axes of the slice: x: 4, y: 4 (y_hi: 2, y_lo: 2; y = y_hi * 2 + y_lo), z: 8, core: 2. Of those that a mesh axis runs over, the one named last changes fastest.
Arguments:
- velocity: float32 [3, 1024, 32, 2048], P(None, 'gx', None, 'gz'), may hold values from -4 to 4
Outputs:
- new_velocity: float32 [3, 1024, 32, 2048], P(None, 'gx', None, 'gz')
- nonlinear: float32 [3, 1024, 32, 2048], P(None, 'gx', None, 'gz')
All inputs are finite; a program needn't handle non-finite values.
Results may differ from a plain program's by a relative error of at most 0.0008.
Values sent between devices are 32-bit elements; how exact they have to be, the bound alone decides.
No kernel may reach another device: no remote copies, remote signals or barrier semaphores. Data moves between devices by JAX's collectives and lax.ppermute only.
A program may use at most 128 MiB of HBM per device.

v0:
```python
import jax
import jax.numpy as jnp
from jax import lax
from jax.sharding import PartitionSpec as P

VISC = 12288


courant = 0.1


def extended(block, sides, width):
    for axis, dim in sides:
        count = lax.axis_size(axis)
        forward = [(i, i + 1) for i in range(count - 1)]
        forward.append((count - 1, 0))
        backward = [(target, source) for source, target in forward]
        low = lax.ppermute(
            lax.slice_in_dim(block, block.shape[dim] - width, None, axis=dim), axis, forward
        )
        high = lax.ppermute(lax.slice_in_dim(block, 0, width, axis=dim), axis, backward)
        block = jnp.concatenate([low, block, high], axis=dim)
    return block


def passed_along(value, axis, steps):
    count = lax.axis_size(axis)
    pairs = [(source, (source + steps) % count) for source in range(count)]
    return lax.ppermute(value, axis, pairs)


def centred(lower_two, lower_one, upper_one, upper_two):
    return (8.0 * (upper_one - lower_one) - (upper_two - lower_two)) / 12.0


def build_tables(x_cells, cycle_size, visc):
    inner_size = x_cells - 1
    value = float(visc)
    period = 2 * (inner_size + 1)
    counter = jnp.arange(1, inner_size + 1, dtype=jnp.int32)
    products = counter[:, None] * counter[None, :] % period
    angle_unit = jnp.pi / (inner_size + 1)
    basis = jnp.sqrt(2.0 / (inner_size + 1)) * jnp.sin(products.astype(jnp.float32) * angle_unit)
    eigen = 1.0 + 4.0 * value * jnp.sin(counter.astype(jnp.float32) * (0.5 * angle_unit)) ** 2
    inverse_block = jnp.dot(basis / eigen[None, :], basis.T, precision=lax.Precision.HIGHEST)
    centre_term = 1.0 + 2.0 * value - value * value * (inverse_block[0, 0] + inverse_block[-1, -1])
    side_term = -value * value * inverse_block[0, -1]
    cycle_index = jnp.arange(cycle_size, dtype=jnp.int32)
    phase = (cycle_index[:, None] * cycle_index[None, :] % cycle_size).astype(jnp.float32)
    cosines = jnp.cos(2.0 * jnp.pi * phase / cycle_size)
    denominator = centre_term + 2.0 * side_term * jnp.cos(
        2.0 * jnp.pi * cycle_index.astype(jnp.float32) / cycle_size
    )
    profile = jnp.sum(cosines / denominator[None, :], axis=1) / cycle_size
    offsets = (cycle_index[:, None] - cycle_index[None, :]) % cycle_size
    schur_inverse = jnp.take(profile, offsets, axis=0)
    row_pairs = jnp.stack([jnp.roll(schur_inverse, 1, axis=0), schur_inverse], axis=1)
    full_inverse = jnp.pad(inverse_block, ((0, 1), (0, 1)))
    return (full_inverse, schur_inverse, row_pairs)


def shards(velocity):
    x_cells = velocity.shape[1]
    y_cells = velocity.shape[2]
    z_cells = velocity.shape[3]
    cycle_size = lax.axis_size("gx")
    padded = extended(velocity, (("gx", 1), ("gz", 3)), 2)
    along_x = padded[:, :, :, 2 : z_cells + 2]
    along_z = padded[:, 2 : x_cells + 2]
    grad_x = centred(
        along_x[:, 0:x_cells],
        along_x[:, 1 : x_cells + 1],
        along_x[:, 3 : x_cells + 3],
        along_x[:, 4 : x_cells + 4],
    )
    grad_z = centred(
        along_z[..., 0:z_cells],
        along_z[..., 1 : z_cells + 1],
        along_z[..., 3 : z_cells + 3],
        along_z[..., 4 : z_cells + 4],
    )
    wrapped = jnp.concatenate([velocity[:, :, y_cells - 2 :], velocity, velocity[:, :, :2]], axis=2)
    grad_y = centred(
        wrapped[:, :, 0:y_cells],
        wrapped[:, :, 1 : y_cells + 1],
        wrapped[:, :, 3 : y_cells + 3],
        wrapped[:, :, 4 : y_cells + 4],
    )
    nonlinear = velocity[0][None] * grad_x + velocity[1][None] * grad_y + velocity[2][None] * grad_z
    laplace = along_x[:, 3 : x_cells + 3] - 2.0 * velocity + along_x[:, 1 : x_cells + 1]
    rhs = velocity + VISC * laplace - courant * nonlinear
    inner_size = x_cells - 1
    line_count = y_cells * z_cells
    full_inverse, schur_inverse, row_pairs = build_tables(x_cells, cycle_size, VISC)
    rhs_lines = rhs.reshape(3, x_cells, line_count)
    local_part = jnp.stack(
        [
            jnp.dot(full_inverse, rhs_lines[comp], precision=lax.Precision.HIGHEST)
            for comp in range(3)
        ],
        axis=0,
    )
    edge_rows = rhs_lines[:, inner_size]
    next_first = passed_along(local_part[:, 0], "gx", -1)
    reduced = edge_rows + VISC * local_part[:, inner_size - 1] + VISC * next_first
    weights = lax.dynamic_index_in_dim(row_pairs, lax.axis_index("gx"), 0, keepdims=False)
    piece = lax.all_gather(reduced[None], "gx", axis=0, tiled=True)
    flat = piece.reshape(piece.shape[0], 3 * line_count)
    both = jnp.dot(weights, flat, precision=lax.Precision.HIGHEST)
    before = both[0].reshape(3, line_count)
    here = both[1].reshape(3, line_count)
    first_column = full_inverse[:, 0]
    last_column = full_inverse[:, inner_size - 1]
    last_unit = (jnp.arange(x_cells, dtype=jnp.int32) == inner_size).astype(jnp.float32)
    solved = (
        local_part
        + VISC * before[:, None] * first_column[None, :, None]
        + (VISC * last_column + last_unit)[None, :, None] * here[:, None]
    )
    new_velocity = solved.reshape(3, x_cells, y_cells, z_cells)
    return (new_velocity, nonlinear)


def solution(mesh):
    in_specs = (P(None, "gx", None, "gz"),)
    out_specs = (P(None, "gx", None, "gz"), P(None, "gx", None, "gz"))
    return jax.shard_map(shards, mesh=mesh, in_specs=in_specs, out_specs=out_specs, check_vma=False)
```

profile of v0, /device:TPU:1, one launch (start us, length us, event | category | flops | bytes accessed | tf_op | source)
XLA Modules:
  0.0 200.0 jit_solution(15027227919110868666)
XLA Ops:
  0.6 0.0 copy-start.1
  0.6 1.8 fusion.89
  2.4 3.2 %collective-permute-start = (f32[3,2,32,128]{3,2,1,0:T(8,128)}, f32[3,2,32,128]{3,2,1,0:T(8,128)}, u32[]{:S(2)}, u32[]{:S(2)}) collective-permute-start(f32[3,2,32,128]{3,2,1,0:T(8,128)} %get-tuple-element.27), channel_id=1, source_target_pairs={{16,0},{32,16},{48,32},{64,48},{80,64},{96,80},{112,96},{128,112},... | collective-permute-start | bytes 294920 | tf_op jit(solution)/shard_map/ppermute | solution.py:21
  5.7 0.0 collective-permute-start.1
  5.7 7.6 %copy.78 = f32[3,64,32,128]{1,2,3,0:T(8,128)} copy(f32[3,64,32,128]{3,2,1,0:T(8,128)} %param.1) | data formatting | bytes 6291456 | tf_op args[0]
  13.2 0.0 copy-done.1
  13.2 1.8 multiply_bitcast_fusion.2
  15.1 0.5 fusion.28
  15.6 0.0 copy-start.7
  15.6 0.7 fusion.90
  18.2 0.2 fusion.64
  18.4 0.1 reshape.239
  18.5 1.9 gather_fusion
  20.4 0.1 reshape.238
  20.5 0.1 gather.7
  20.5 2.9 %fusion.88 = (f32[3,64,2,128]{1,2,3,0:T(2,128)S(1)}, f32[3,64,2,128]{1,2,3,0:T(2,128)}) fusion(f32[3,64,32,128]{1,2,3,0:T(8,128)} %copy.78), kind=kLoop, calls=%fused_computation.148 | loop fusion | bytes 786432 | tf_op jit(solution)/shard_map/slice | solution.py:82
  23.6 0.0 collective-permute-done
  23.6 6.8 %copy.74 = f32[3,2,32,128]{1,2,3,0:T(8,128)} copy(f32[3,2,32,128]{3,2,1,0:T(8,128)} %collective-permute-done) | data formatting | bytes 196608 | tf_op jit(solution)/shard_map/ppermute | solution.py:21
  30.4 0.0 collective-permute-done.1
  30.4 6.7 %copy.76 = f32[3,2,32,128]{1,2,3,0:T(8,128)} copy(f32[3,2,32,128]{3,2,1,0:T(8,128)} %collective-permute-done.1) | data formatting | bytes 196608 | tf_op jit(solution)/shard_map/ppermute | solution.py:18
  37.0 2.0 pad_maximum_fusion.7
  39.0 7.5 %collective-permute-start.2 = (f32[3,68,32,2]{1,2,3,0:T(8,128)}, f32[3,68,32,2]{1,2,3,0:T(8,128)}, u32[]{:S(2)}, u32[]{:S(2)}) collective-permute-start(f32[3,68,32,2]{1,2,3,0:T(8,128)} %get-tuple-element.14), channel_id=1, source_target_pairs={{1,0},{2,1},{3,2},{4,3},{5,4},{6,5},{7,6},{8,7},{9,8},{10,9},{11,1... | collective-permute-start | bytes 156680 | tf_op jit(solution)/shard_map/ppermute | solution.py:21
  46.6 0.0 collective-permute-start.3
  46.6 0.0 copy-done.7
  46.6 0.5 fusion.72
  47.1 3.0 %copy.79 = f32[64,32,128]{0,1,2:T(8,128)S(1)} copy(f32[64,32,128]{2,1,0:T(8,128)} %get-tuple-element.23) | data formatting | bytes 2097152 | tf_op jit(solution)/shard_map/mul | solution.py:89
  50.1 4.1 %copy.84 = f32[64,32,128]{0,1,2:T(8,128)} copy(f32[64,32,128]{2,1,0:T(8,128)} %get-tuple-element.24) | data formatting | bytes 2097152 | tf_op jit(solution)/shard_map/mul | solution.py:89
  54.2 0.0 copy-done.5
  54.2 2.9 %copy.88 = f32[64,32,128]{0,1,2:T(8,128)} copy(f32[64,32,128]{2,1,0:T(8,128)S(1)} %copy-done.5) | data formatting | bytes 2097152 | tf_op jit(solution)/shard_map/mul | solution.py:89
  57.1 0.0 collective-permute-done.2
  57.1 0.0 collective-permute-done.3
  57.1 20.6 %pad_maximum_fusion = (f32[3,68,32,130]{1,2,3,0:T(8,128)}, f32[3,68,32,130]{1,2,3,0:T(8,128)}) fusion(f32[3,68,32,2]{1,2,3,0:T(8,128)} %collective-permute-done.2, f32[3,2,32,128]{1,2,3,0:T(8,128)} %copy.74, f32[3,64,32,128]{1,2,3,0:T(8,128)} %copy.78, f32[3,2,32,128]{1,2,3,0:T(8,128)} %copy.76, f32[3,68,32,2]{1,2,3,0:T(8,128)} %collective-permute-done.3), kind=kLoop, calls=%fused_computation.5 | loop fusion | flops 5091840 | bytes 10235904 | tf_op jit(solution)/shard_map/concatenate | solution.py:22
  77.7 0.0 copy-done.6
  77.7 50.2 %multiply_subtract_fusion = (f32[3,64,32,128]{1,2,3,0:T(8,128)S(1)}, f32[3,64,32,128]{1,2,3,0:T(8,128)}) fusion(f32[3,64,32,128]{1,2,3,0:T(8,128)} %copy.78, f32[3,2,32,128]{1,2,3,0:T(8,128)} %copy.74, f32[3,2,32,128]{1,2,3,0:T(8,128)} %copy.76, f32[64,32,128]{0,1,2:T(8,128)} %copy.88, f32[3,68,32,130]{1,2,3,0:T(8,128)} %get-tuple-element.13, ...), kind=kLoop, calls=%fused_computation.30 | loop fusion | flops 26738688 | bytes 25755648 | tf_op jit(solution)/shard_map/sub | solution.py:91
  127.9 0.0 copy-start
  127.9 0.0 copy-start.8
  128.0 3.2 %fusion.87 = (f32[1,64,32,128]{1,2,3,0:T(8,128)}, f32[1,64,32,128]{1,2,3,0:T(8,128)}, f32[1,64,32,128]{1,2,3,0:T(8,128)S(1)}) fusion(f32[3,64,32,128]{1,2,3,0:T(8,128)S(1)} %get-tuple-element.10), kind=kLoop, calls=%fused_computation.147 | loop fusion | bytes 6291456 | tf_op jit(solution)/shard_map/slice | solution.py:98
  131.1 0.7 copy-done
  131.8 3.9 %copy.89 = f32[1,64,32,128]{3,2,1,0:T(8,128)} copy(f32[1,64,32,128]{1,2,3,0:T(8,128)} %get-tuple-element.16) | data formatting | bytes 2097152 | tf_op jit(solution)/shard_map/slice | solution.py:98
  135.7 0.0 copy-done.8
  135.7 2.8 %fusion.22 = f32[64,4096]{1,0:T(8,128)S(1)} fusion(f32[8,8,32,128]{3,2,1,0:T(8,128)} %bitcast.74, f32[63,63]{0,1:T(8,128)S(1)} %copy-done.8), kind=kOutput, calls=%fused_computation.39 | convolution fusion | flops 201326592 | bytes 2113028 | tf_op jit(solution)/shard_map/dot_general | solution.py:98
  138.5 0.0 copy-start.2
  138.5 2.5 %copy.90 = f32[1,64,32,128]{3,2,1,0:T(8,128)} copy(f32[1,64,32,128]{1,2,3,0:T(8,128)S(1)} %get-tuple-element.18) | data formatting | bytes 2097152 | tf_op jit(solution)/shard_map/slice | solution.py:98
  141.0 2.8 %fusion.19 = f32[64,4096]{1,0:T(8,128)S(1)} fusion(f32[8,8,32,128]{3,2,1,0:T(8,128)} %bitcast.75, f32[63,63]{0,1:T(8,128)S(1)} %copy-done.8), kind=kOutput, calls=%fused_computation.36 | convolution fusion | flops 201326592 | bytes 2113028 | tf_op jit(solution)/shard_map/dot_general | solution.py:98
  143.8 3.4 %copy.91 = f32[1,64,32,128]{3,2,1,0:T(8,128)S(1)} copy(f32[1,64,32,128]{1,2,3,0:T(8,128)} %get-tuple-element.17) | data formatting | bytes 2097152 | tf_op jit(solution)/shard_map/slice | solution.py:98
  147.2 1.6 fusion.16
  148.8 0.0 copy-start.4
  148.9 0.1 pad_maximum_fusion.8
  148.9 0.9 copy-done.4
  149.9 2.2 %collective-permute-start.4 = (f32[3,4096]{1,0:T(4,128)S(1)}, f32[3,4096]{1,0:T(4,128)S(1)}, u32[]{:S(2)}, u32[]{:S(2)}) collective-permute-start(f32[3,4096]{1,0:T(4,128)S(1)} %bitcast.84), channel_id=1, source_target_pairs={{0,240},{16,0},{32,16},{48,32},{64,48},{80,64},{96,80},{112,96},{1... | collective-permute-start | bytes 147464 | tf_op jit(solution)/shard_map/ppermute | solution.py:29
  152.1 6.3 %copy.96 = f32[3,64,32,128]{3,2,0,1:T(8,128)S(1)} copy(f32[3,64,32,128]{1,2,3,0:T(8,128)} %copy-done) | data formatting | bytes 6291456 | tf_op jit(solution)/shard_map/reshape | solution.py:95
  158.4 2.9 %reshape.252 = f32[3,64,4096]{2,0,1:T(4,128)} reshape(f32[3,64,32,128]{3,2,0,1:T(8,128)S(1)} %copy.96) | data formatting | bytes 6291456 | tf_op jit(solution)/shard_map/reshape | solution.py:95
  161.4 1.4 copy.101
  162.8 1.4 copy.103
  164.2 1.4 copy.105
  165.6 0.0 copy-start.9
  165.6 7.2 %copy.95 = f32[3,64,32,128]{3,2,1,0:T(8,128)} copy(f32[3,64,32,128]{1,2,3,0:T(8,128)} %get-tuple-element.11) | data formatting | bytes 6291456
  172.8 0.0 collective-permute-done.4
  172.8 0.9 fusion.27
  173.7 23.0 %all-gather.1 = f32[16,3,4096]{2,1,0:T(4,128)S(1)} all-gather(f32[1,3,4096]{2,1,0:T(4,128)S(1)} %fusion.27), channel_id=2, replica_groups=mesh['gx'=16,'gz'=16] {'gx'}, dimensions={0}, use_global_device_ids=true | all-gather | bytes 835584 | tf_op jit(solution)/shard_map/all_gather | solution.py:107
  196.7 0.5 copy.106
  197.2 0.5 fusion.69
  197.7 0.1 slice_multiply_fusion
  197.8 2.2 %fusion.15 = f32[3,64,32,128]{3,2,1,0:T(8,128)} fusion(f32[1,64,32,128]{3,2,1,0:T(8,128)S(1)} %bitcast.80, f32[1,64,32,128]{3,2,1,0:T(8,128)S(1)} %bitcast.79, f32[1,64,32,128]{3,2,1,0:T(8,128)S(1)} %bitcast.78, f32[3,32,128]{2,1,0:T(8,128)S(1)} %bitcast.83, f32[64]{0:T(128)S(1)} %copy-done.9, f32[64]{0:T(128)S(1)} %fusion.73, f32[3,32,128]{2,1,0:T(8,128)S(1)} %bitcast.82), kind=kLoop, calls=%fused_computation.32 | loop fusion | flops 4718592 | bytes 6390272 | tf_op jit(solution)/shard_map/add | solution.py:116
  (18 shorter events, 0.3 us)
Async XLA Ops:
  0.6 12.6 %copy-start.1 = (f32[3,64,32,128]{3,2,1,0:T(8,128)S(1)}, f32[3,64,32,128]{3,2,1,0:T(8,128)}, u32[]{:S(2)}) copy-start(f32[3,64,32,128]{3,2,1,0:T(8,128)} %param.1) | copy-start | bytes 9437188
  2.4 21.2 %collective-permute-start = (f32[3,2,32,128]{3,2,1,0:T(8,128)}, f32[3,2,32,128]{3,2,1,0:T(8,128)}, u32[]{:S(2)}, u32[]{:S(2)}) collective-permute-start(f32[3,2,32,128]{3,2,1,0:T(8,128)} %get-tuple-element.27), channel_id=1, source_target_pairs={{16,0},{32,16},{48,32},{64,48},{80,64},{96,80},{112,96},{128,112},... | collective-permute-start | bytes 294920 | tf_op jit(solution)/shard_map/ppermute | solution.py:21
  5.7 24.7 %collective-permute-start.1 = (f32[3,2,32,128]{3,2,1,0:T(8,128)}, f32[3,2,32,128]{3,2,1,0:T(8,128)}, u32[]{:S(2)}, u32[]{:S(2)}) collective-permute-start(f32[3,2,32,128]{3,2,1,0:T(8,128)} %get-tuple-element.26), channel_id=1, source_target_pairs={{0,16},{16,32},{32,48},{48,64},{64,80},{80,96},{96,112},{112,128},... | collective-permute-start | bytes 294920 | tf_op jit(solution)/shard_map/ppermute | solution.py:18
  15.6 31.0 %copy-start.7 = (f32[63,63]{0,1:T(8,128)}, f32[63,63]{0,1:T(8,128)S(1)}, u32[]{:S(2)}) copy-start(f32[63,63]{0,1:T(8,128)S(1)} %fusion.28) | copy-start | bytes 47632
  39.0 15.2 %copy-start.5 = (f32[64,32,128]{2,1,0:T(8,128)S(1)}, f32[64,32,128]{2,1,0:T(8,128)}, u32[]{:S(2)}) copy-start(f32[64,32,128]{2,1,0:T(8,128)} %get-tuple-element.25) | copy-start | bytes 3145732
  39.0 18.1 %collective-permute-start.2 = (f32[3,68,32,2]{1,2,3,0:T(8,128)}, f32[3,68,32,2]{1,2,3,0:T(8,128)}, u32[]{:S(2)}, u32[]{:S(2)}) collective-permute-start(f32[3,68,32,2]{1,2,3,0:T(8,128)} %get-tuple-element.14), channel_id=1, source_target_pairs={{1,0},{2,1},{3,2},{4,3},{5,4},{6,5},{7,6},{8,7},{9,8},{10,9},{11,1... | collective-permute-start | bytes 156680 | tf_op jit(solution)/shard_map/ppermute | solution.py:21
  46.6 10.6 %collective-permute-start.3 = (f32[3,68,32,2]{1,2,3,0:T(8,128)}, f32[3,68,32,2]{1,2,3,0:T(8,128)}, u32[]{:S(2)}, u32[]{:S(2)}) collective-permute-start(f32[3,68,32,2]{1,2,3,0:T(8,128)} %get-tuple-element.15), channel_id=1, source_target_pairs={{0,1},{1,2},{2,3},{3,4},{4,5},{5,6},{6,7},{7,8},{8,9},{9,10},{10,1... | collective-permute-start | bytes 156680 | tf_op jit(solution)/shard_map/ppermute | solution.py:18
  57.1 20.6 %copy-start.6 = (f32[3,64,2,128]{1,2,3,0:T(2,128)S(1)}, f32[3,64,2,128]{1,2,3,0:T(2,128)}, u32[]{:S(2)}) copy-start(f32[3,64,2,128]{1,2,3,0:T(2,128)} %get-tuple-element.20) | copy-start | bytes 589828
  127.9 3.9 %copy-start = (f32[3,64,32,128]{1,2,3,0:T(8,128)}, f32[3,64,32,128]{1,2,3,0:T(8,128)S(1)}, u32[]{:S(2)}) copy-start(f32[3,64,32,128]{1,2,3,0:T(8,128)S(1)} %get-tuple-element.10) | copy-start | bytes 9437188
  127.9 7.7 %copy-start.8 = (f32[63,63]{0,1:T(8,128)S(1)}, f32[63,63]{0,1:T(8,128)}, u32[]{:S(2)}) copy-start(f32[63,63]{0,1:T(8,128)} %copy-done.7) | copy-start | bytes 47632
  138.5 10.5 %copy-start.2 = (f32[64,4096]{1,0:T(8,128)}, f32[64,4096]{1,0:T(8,128)S(1)}, u32[]{:S(2)}) copy-start(f32[64,4096]{1,0:T(8,128)S(1)} %fusion.22) | copy-start | bytes 3145732
  143.8 8.2 %copy-start.3 = (f32[64,4096]{1,0:T(8,128)}, f32[64,4096]{1,0:T(8,128)S(1)}, u32[]{:S(2)}) copy-start(f32[64,4096]{1,0:T(8,128)S(1)} %fusion.19) | copy-start | bytes 3145732
  148.8 1.0 copy-start.4
  149.9 23.0 %collective-permute-start.4 = (f32[3,4096]{1,0:T(4,128)S(1)}, f32[3,4096]{1,0:T(4,128)S(1)}, u32[]{:S(2)}, u32[]{:S(2)}) collective-permute-start(f32[3,4096]{1,0:T(4,128)S(1)} %bitcast.84), channel_id=1, source_target_pairs={{0,240},{16,0},{32,16},{48,32},{64,48},{80,64},{96,80},{112,96},{1... | collective-permute-start | bytes 147464 | tf_op jit(solution)/shard_map/ppermute | solution.py:29
  165.6 32.2 %copy-start.9 = (f32[64]{0:T(128)S(1)}, f32[64]{0:T(128)}, u32[]{:S(2)}) copy-start(f32[64]{0:T(128)} %fusion.72) | copy-start | bytes 772
where the time goes:
time: 201 us; the launch traced here: 200 us
  other arithmetic  78.7 us (39%)
  local copies, waits for them, and re-layouts  74.3 us (37%)
  blocking collectives  23 us (11%)
  starting transfers between devices  13 us (6%)
  matrix products  8.19 us (4%)
  between operations  2.81 us (1%)
    sub x1, other arithmetic, shards(): rhs = velocity + VISC * laplace - courant * nonlinear  50.2 us
    all_gather x1, blocking collectives, shards(): piece = lax.all_gather(reduced[None], 'gx', axis=0, tiled=True)  23 us
    unnamed x27, local copies, waits for them, and re-layouts  21.1 us
    concatenate x1, other arithmetic, extended(): block = jnp.concatenate([low, block, high], axis=dim)  20.6 us
    slice x4, local copies, waits for them, and re-layouts, shards(): rhs_lines[comp]  13 us
    ppermute x2, starting transfers between devices, extended(): lax.ppermute(lax.slice_in_dim(block, 0, width, axis=dim), axis, backward)  10.8 us
    reshape x2, local copies, waits for them, and re-layouts, shards(): rhs_lines = rhs.reshape(3, x_cells, line_count)  9.29 us
    dot_general x3, matrix products, shards(): jnp.dot(full_inverse, rhs_lines[comp], precision=lax.Precision.HIGHEST)  7.2 us
  transfers between devices with their start and end apart: 5, of which 0 were waited for; matrix products, arithmetic and copies ran while one was open for 27% of the time, Pallas kernels for 0%

commit v1 on v0

v1 whole, which is shorter than its diff:
```python
import math

import jax
import jax.numpy as jnp
from jax import lax
from jax.experimental import pallas as pl
from jax.experimental.pallas import tpu as pltpu
from jax.sharding import PartitionSpec as P

VISC = 12288
COURANT = 0.1

HALF = 1.0 / (2.0 * VISC)
LAM = 1.0 + HALF - math.sqrt(2.0 * HALF + HALF * HALF)
GAIN = 1.0 / (1.0 + 2.0 * VISC * (1.0 - LAM))

X = 64
Y = 32
Z = 128
CHUNK = 8
CHUNKS = X // CHUNK
CHIPS = 8
PERIOD = 2 * X * CHIPS
F32 = jnp.float32
VM = pl.BlockSpec(memory_space=pltpu.VMEM)
ANY = pl.BlockSpec(memory_space=pl.ANY)


def params(mib):
    return pltpu.CompilerParams(vmem_limit_bytes=mib * 1024 * 1024)


def shape(*dims):
    return jax.ShapeDtypeStruct(dims, F32)


def lanes(rows):
    return lax.broadcasted_iota(jnp.int32, (rows, Z), 1)


def shift(a, amount):
    return pltpu.roll(a, amount % Z, 1)


def pack_kernel(v_ref, xa_ref, xb_ref, za_ref, zb_ref):
    px = lax.rem(lax.axis_index("gx"), 2)
    pz = lax.rem(lax.axis_index("gz"), 2)
    first = (1 - px) * (X - 2)
    xa_ref[...] = v_ref[:, pl.ds(first, 2)]
    xb_ref[...] = v_ref[:, pl.ds(X - 2 - first, 2)]
    slot = lanes(3 * Y) >> 1

    def body(x, carry):
        bottom, top = carry
        turned = pltpu.roll(v_ref[:, x].reshape(3 * Y, Z), 2 * x, 1)
        bottom = jnp.where(slot == x, turned, bottom)
        top = jnp.where(slot == lax.rem(x + X - 1, X), turned, top)
        return bottom, top

    zero = jnp.zeros((3 * Y, Z), F32)
    bottom, top = lax.fori_loop(0, X, body, (zero, zero), unroll=4)
    even = pz == 0
    za_ref[...] = jnp.where(even, top, bottom).reshape(3, Y, Z)
    zb_ref[...] = jnp.where(even, bottom, top).reshape(3, Y, Z)


def stencil_kernel(
    v_ref, xa_ref, xb_ref, za_ref, zb_ref, ra_ref, rb_ref,
    n_ref, u_ref, mom_ref,
    vp, nb, pb, edge, vsem, nsem, usem,
):
    def v_copy(j):
        rows = pl.ds(j * CHUNK, CHUNK)
        return pltpu.make_async_copy(v_ref.at[:, rows], vp.at[:, pl.ds(2 + j * CHUNK, CHUNK)], vsem.at[j])

    def n_copy(j):
        rows = pl.ds(j * CHUNK, CHUNK)
        return pltpu.make_async_copy(nb.at[:, rows], n_ref.at[:, rows], nsem.at[j])

    def u_copy(j):
        rows = pl.ds(j * CHUNK, CHUNK)
        return pltpu.make_async_copy(pb.at[:, rows], u_ref.at[:, rows], usem.at[j])

    for j in range(CHUNKS):
        v_copy(j).start()
    x_even = lax.rem(lax.axis_index("gx"), 2) == 0
    z_even = lax.rem(lax.axis_index("gz"), 2) == 0
    vp[:, 0:2] = jnp.where(x_even, xb_ref[...], xa_ref[...])
    vp[:, X + 2 : X + 4] = jnp.where(x_even, xa_ref[...], xb_ref[...])

    lane = lanes(3 * Y)
    even_lane = lane & 1 == 0
    own_top = jnp.where(z_even, za_ref[...], zb_ref[...])
    own_bottom = jnp.where(z_even, zb_ref[...], za_ref[...])
    high = (jnp.where(z_even, ra_ref[...], rb_ref[...]) - own_bottom).reshape(3 * Y, Z)
    low = (jnp.where(z_even, rb_ref[...], ra_ref[...]) - own_top).reshape(3 * Y, Z)
    low_two = shift(low, 2)
    at_bottom = jnp.where(even_lane, low_two - 8.0 * shift(low, 1), low_two)
    high_two = shift(high, -2)
    at_top = jnp.where(even_lane, -high_two, 8.0 * shift(high, -1) - high_two)
    early = lane & 3 < 2
    edge[0] = jnp.where(early, at_bottom, at_top)
    edge[1] = jnp.where(early, at_top, at_bottom)
    border = (lane < 2) | (lane >= Z - 2)

    def forward(x, carry):
        p, q, power = carry
        f = vp[:, x + 2]
        gx = 8.0 * (vp[:, x + 3] - vp[:, x + 1]) - (vp[:, x + 4] - vp[:, x])
        flat = f.reshape(3 * Y, Z)
        one = shift(flat, -1) - shift(flat, 1)
        fix = pltpu.roll(edge[lax.rem(x, 2)], lax.rem(2 * (X - x), Z), 1)
        gz = 8.0 * one - (shift(one, -1) + shift(one, 1)) + jnp.where(border, fix, 0.0)
        gz = gz.reshape(3, Y, Z)
        step = pltpu.roll(f, Y - 1, 1) - pltpu.roll(f, 1, 1)
        gy = 8.0 * step - (pltpu.roll(step, Y - 1, 1) + pltpu.roll(step, 1, 1))
        u = f * (1.0 / 12.0)
        n = u[0][None] * gx + u[1][None] * gy + u[2][None] * gz
        w = 2.0 * f - COURANT * n
        p = LAM * p + w
        q = q + power * w
        nb[:, x] = n
        pb[:, x] = p
        return p, q, power * LAM

    zero = jnp.zeros((3, Y, Z), F32)
    carry = (zero, zero, F32(1.0))
    v_copy(0).wait()
    for j in range(CHUNKS):
        if j + 1 < CHUNKS:
            v_copy(j + 1).wait()
        carry = lax.fori_loop(j * CHUNK, (j + 1) * CHUNK, forward, carry)
        n_copy(j).start()
    mom_ref[0] = carry[0]
    mom_ref[1] = carry[1]

    def backward(k, q, j):
        x = (j + 1) * CHUNK - 1 - k
        f = vp[:, x + 2]
        w = 2.0 * f - COURANT * nb[:, x]
        q = LAM * q
        pb[:, x] = GAIN * (pb[:, x] + q) - f
        return q + w

    q = zero
    for j in reversed(range(CHUNKS)):
        q = lax.fori_loop(0, CHUNK, lambda k, q, j=j: backward(k, q, j), q)
        u_copy(j).start()
    for j in range(CHUNKS):
        n_copy(j).wait()
        u_copy(j).wait()


def chip_kernel(own_ref, other_ref, out_ref):
    core = lax.rem(lax.axis_index("gx"), 2)
    rows = pl.ds(pl.multiple_of(core * (Y // 2), Y // 2), Y // 2)
    own_p, own_q = own_ref[0, :, rows], own_ref[1, :, rows]
    other_p, other_q = other_ref[0, :, rows], other_ref[1, :, rows]
    first = core == 0
    far = LAM**X
    p = jnp.where(first, own_p, other_p) * far + jnp.where(first, other_p, own_p)
    q = jnp.where(first, own_q, other_q) + far * jnp.where(first, other_q, own_q)
    for k in range(CHIPS):
        out_ref[k, 0] = p
        out_ref[k, 1] = q


def join_kernel(all_ref, out_ref):
    chip = lax.div(lax.axis_index("gx"), 2)
    p = jnp.zeros(all_ref.shape[2:], F32)
    q = p
    for s in range(1, CHIPS + 1):
        weight = LAM ** (2 * X * (s - 1)) / (1.0 - LAM**PERIOD)
        p = p + weight * all_ref[lax.rem(chip + CHIPS - s % CHIPS, CHIPS), 0]
        q = q + weight * all_ref[lax.rem(chip + s, CHIPS), 1]
    out_ref[0] = p
    out_ref[1] = q


def final_kernel(u_ref, in_own_ref, in_other_ref, other_ref, out_ref, ub, ob, isem, osem):
    def i_copy(j):
        rows = pl.ds(j * CHUNK, CHUNK)
        return pltpu.make_async_copy(u_ref.at[:, rows], ub.at[:, rows], isem.at[j])

    def o_copy(j):
        rows = pl.ds(j * CHUNK, CHUNK)
        return pltpu.make_async_copy(ob.at[:, rows], out_ref.at[:, rows], osem.at[j])

    for j in range(CHUNKS):
        i_copy(j).start()
    first = lax.rem(lax.axis_index("gx"), 2) == 0
    own, other = in_own_ref[...], in_other_ref[...]
    both = jnp.concatenate([jnp.where(first, own, other), jnp.where(first, other, own)], axis=2)
    far = LAM**X
    p_in = jnp.where(first, both[0], other_ref[0] + far * both[0])
    q_in = jnp.where(first, other_ref[1] + far * both[1], both[1])

    def body(x, carry):
        p, q = carry
        ob[:, x] = ub[:, x] + (p + q)
        return p * LAM, q * (1.0 / LAM)

    carry = ((GAIN * LAM) * p_in, (GAIN * far) * q_in)
    for j in range(CHUNKS):
        i_copy(j).wait()
        carry = lax.fori_loop(j * CHUNK, (j + 1) * CHUNK, body, carry)
        o_copy(j).start()
    for j in range(CHUNKS):
        o_copy(j).wait()


def pair_low(count):
    return [(i, i ^ 1) for i in range(count)]


def pair_high(count):
    return [(i, (i + 1 if i % 2 else i - 1) % count) for i in range(count)]


def shards(v):
    nx, nz = lax.axis_size("gx"), lax.axis_size("gz")
    sems = [pltpu.SemaphoreType.DMA((CHUNKS,))]
    xa, xb, za, zb = pl.pallas_call(
        pack_kernel,
        out_shape=[shape(3, 2, Y, Z)] * 2 + [shape(3, Y, Z)] * 2,
        in_specs=[VM],
        out_specs=[VM] * 4,
        compiler_params=params(16),
        name="pack",
    )(v)
    rzb = lax.ppermute(zb, "gz", pair_high(nz))
    rza = lax.ppermute(za, "gz", pair_low(nz))
    rxb = lax.ppermute(xb, "gx", pair_high(nx))
    rxa = lax.ppermute(xa, "gx", pair_low(nx))
    n, u, mom = pl.pallas_call(
        stencil_kernel,
        out_shape=[shape(3, X, Y, Z), shape(3, X, Y, Z), shape(2, 3, Y, Z)],
        in_specs=[ANY] + [VM] * 6,
        out_specs=[ANY, ANY, VM],
        scratch_shapes=[
            pltpu.VMEM((3, X + 4, Y, Z), F32),
            pltpu.VMEM((3, X, Y, Z), F32),
            pltpu.VMEM((3, X, Y, Z), F32),
            pltpu.VMEM((2, 3 * Y, Z), F32),
        ]
        + sems * 3,
        compiler_params=params(24),
        name="stencil",
    )(v, rxa, rxb, za, zb, rza, rzb)
    other = lax.ppermute(mom, "gx", pair_low(nx))
    half = (2, 3, Y // 2, Z)
    chip = pl.pallas_call(
        chip_kernel,
        out_shape=shape(CHIPS, *half),
        in_specs=[VM, VM],
        out_specs=VM,
        compiler_params=params(16),
        name="chip",
    )(mom, other)
    groups = [[core + 2 * k for k in range(CHIPS)] for core in range(2)]
    everyone = lax.all_to_all(chip, "gx", 0, 0, axis_index_groups=groups)
    joined = pl.pallas_call(
        join_kernel,
        out_shape=shape(*half),
        in_specs=[VM],
        out_specs=VM,
        compiler_params=params(16),
        name="join",
    )(everyone)
    joined_other = lax.ppermute(joined, "gx", pair_low(nx))
    new = pl.pallas_call(
        final_kernel,
        out_shape=shape(3, X, Y, Z),
        in_specs=[ANY, VM, VM, VM],
        out_specs=ANY,
        scratch_shapes=[pltpu.VMEM((3, X, Y, Z), F32)] * 2 + sems * 2,
        compiler_params=params(16),
        name="final",
    )(u, joined, joined_other, other)
    return new, n


def solution(mesh):
    spec = P(None, "gx", None, "gz")
    return jax.shard_map(shards, mesh=mesh, in_specs=(spec,), out_specs=(spec, spec), check_vma=False)
```

time: 201 us -> 52.8 us (0.26)
  other arithmetic: 78.7 us -> 0 us
  local copies, waits for them, and re-layouts: 74.3 us -> 1.89 us
  Pallas kernels: 0 us -> 19.5 us
  blocking collectives: 23 us -> 10.3 us
  matrix products: 8.19 us -> 0 us
  starting transfers between devices: 13 us -> 17 us
  waiting for transfers between devices: 0.01 us -> 3.31 us
  between operations: 2.81 us -> 0.67 us
    sub x1 -> x0, other arithmetic: 50.2 us -> none  [shards(): rhs = velocity + VISC * laplace - courant * nonlinear]
    all_gather x1 -> x0, blocking collectives: 23 us -> none  [shards(): piece = lax.all_gather(reduced[None], 'gx', axis=0, tiled=True)]
    concatenate x2 -> x0, other arithmetic: 20.6 us -> none  [the longest x1 20.6 us: extended(): block = jnp.concatenate([low, block, high], axis=dim)]
    pallas_call x0 -> x5, Pallas kernels: none -> 19.5 us  [the longest x1 15 us: shards(): pl.pallas_call(stencil_kernel, out_shape=[shape(3, X, Y, Z), shape(3, X,...]
    unnamed x27 -> x4, local copies, waits for them, and re-layouts: 21.1 us -> 1.89 us
    slice x8 -> x0, local copies, waits for them, and re-layouts: 18.4 us -> none  [the longest x4 13 us: shards(): rhs_lines[comp]]
    ppermute x2 -> x0, local copies, waits for them, and re-layouts: 13.4 us -> none  [the longest x1 6.77 us: extended(): lax.ppermute(lax.slice_in_dim(block, 0, width, axis=dim), axis, backward)]
    all_to_all x0 -> x1, blocking collectives: none -> 10.3 us  [shards(): everyone = lax.all_to_all(chip, 'gx', 0, 0, axis_index_groups=groups)]
  transfers between devices with their start and end apart: 5 -> 6, of which waited for: 0 -> 3; matrix products, arithmetic and copies ran while one was open for 27% -> 0% of each run, Pallas kernels for 0% -> 0%
where the time goes in v1:
time: 52.8 us; the launch traced here: 52.7 us
  Pallas kernels  19.5 us (37%)
  starting transfers between devices  17 us (32%)
  blocking collectives  10.3 us (20%)
  waiting for transfers between devices  3.31 us (6%)
  local copies, waits for them, and re-layouts  1.89 us (4%)
  between operations  0.67 us (1%)
    pallas_call x1, Pallas kernels, shards(): pl.pallas_call(stencil_kernel, out_shape=[shape(3, X, Y, Z), shape(3, X,...  15 us
    all_to_all x1, blocking collectives, shards(): everyone = lax.all_to_all(chip, 'gx', 0, 0, axis_index_groups=groups)  10.3 us
    ppermute x1, starting transfers between devices, shards(): rzb = lax.ppermute(zb, 'gz', pair_high(nz))  7 us
    ppermute x1, starting transfers between devices, shards(): other = lax.ppermute(mom, 'gx', pair_low(nx))  3.84 us
    ppermute x1, starting transfers between devices, shards(): rxa = lax.ppermute(xa, 'gx', pair_low(nx))  3.33 us
    pallas_call x1, Pallas kernels, shards(): pl.pallas_call(final_kernel, out_shape=shape(3, X, Y, Z), in_specs=[ANY,...  2.41 us
    pallas_call x1, Pallas kernels, shards(): pl.pallas_call(pack_kernel, out_shape=[shape(3, 2, Y, Z)] * 2 + [shape(3,...  2.01 us
    unnamed x4, local copies, waits for them, and re-layouts  1.89 us
  transfers between devices with their start and end apart: 6, of which 3 were waited for; matrix products, arithmetic and copies ran while one was open for 0% of the time, Pallas kernels for 0%

profile of v1, /device:TPU:1, one launch (start us, length us, event | category | flops | bytes accessed | tf_op | source)
XLA Modules:
  0.0 52.7 jit_solution(18282922645599568058)
XLA Ops:
  0.6 0.0 copy-start
  0.6 1.9 %copy-done = f32[3,64,32,128]{3,2,1,0:T(8,128)S(1)} copy-done((f32[3,64,32,128]{3,2,1,0:T(8,128)S(1)}, f32[3,64,32,128]{3,2,1,0:T(8,128)}, u32[]{:S(2)}) %copy-start) | copy-done | bytes 3145752
  2.5 0.0 copy-start.1
  2.5 2.0 %pack.1 = (f32[3,2,32,128]{3,2,1,0:T(8,128)S(1)}, f32[3,2,32,128]{3,2,1,0:T(8,128)S(1)}, f32[3,32,128]{2,1,0:T(8,128)S(1)}, f32[3,32,128]{2,1,0:T(8,128)S(1)}) custom-call(f32[3,64,32,128]{3,2,1,0:T(8,128)S(1)} %copy-done), custom_call_target="tpu_custom_call" | custom-call | tf_op jit(solution)/shard_map/pack/pallas_call | solution.py:223
  4.5 3.3 %collective-permute-start = (f32[3,2,32,128]{3,2,1,0:T(8,128)S(1)}, f32[3,2,32,128]{3,2,1,0:T(8,128)S(1)}, u32[]{:S(2)}, u32[]{:S(2)}) collective-permute-start(f32[3,2,32,128]{3,2,1,0:T(8,128)S(1)} %get-tuple-element.9), channel_id=1, source_target_pairs={{0,16},{16,0},{32,48},{48,32},{64,80},{80,64},{96,112},{112,96},{1... | collective-permute-start | bytes 294920 | tf_op jit(solution)/shard_map/ppermute | solution.py:234
  7.9 0.0 collective-permute-start.1
  7.9 1.2 %collective-permute-start.2 = (f32[3,32,128]{2,1,0:T(8,128)S(1)}, f32[3,32,128]{2,1,0:T(8,128)S(1)}, u32[]{:S(2)}, u32[]{:S(2)}) collective-permute-start(f32[3,32,128]{2,1,0:T(8,128)S(1)} %get-tuple-element.11.za_ref), channel_id=1, source_target_pairs={{0,1},{1,0},{2,3},{3,2},{4,5},{5,4},{6,7},{7,6},{8,9},{9,8},{10,11... | collective-permute-start | bytes 147464 | tf_op jit(solution)/shard_map/ppermute | solution.py:232
  9.1 7.0 %collective-permute-start.3 = (f32[3,32,128]{2,1,0:T(8,128)S(1)}, f32[3,32,128]{2,1,0:T(8,128)S(1)}, u32[]{:S(2)}, u32[]{:S(2)}) collective-permute-start(f32[3,32,128]{2,1,0:T(8,128)S(1)} %get-tuple-element.12.zb_ref), channel_id=1, source_target_pairs={{0,15},{1,2},{2,1},{3,4},{4,3},{5,6},{6,5},{7,8},{8,7},{9,10},{10,... | collective-permute-start | bytes 147464 | tf_op jit(solution)/shard_map/ppermute | solution.py:231
  16.1 0.0 collective-permute-done.2.ra_ref
  16.1 1.5 %collective-permute-done.3.rb_ref = f32[3,32,128]{2,1,0:T(8,128)S(1)} collective-permute-done((f32[3,32,128]{2,1,0:T(8,128)S(1)}, f32[3,32,128]{2,1,0:T(8,128)S(1)}, u32[]{:S(2)}, u32[]{:S(2)}) %collective-permute-start.3) | collective-permute-done | bytes 49184 | tf_op jit(solution)/shard_map/ppermute | solution.py:231
  17.5 0.0 collective-permute-done.xa_ref
  17.5 0.0 collective-permute-done.1.xb_ref
  17.5 0.0 copy-done.1
  17.5 15.0 %stencil.1 = (f32[3,64,32,128]{3,2,1,0:T(8,128)}, f32[3,64,32,128]{3,2,1,0:T(8,128)S(1)}, f32[2,3,32,128]{3,2,1,0:T(8,128)S(1)}) custom-call(f32[3,64,32,128]{3,2,1,0:T(8,128)S(1)} %copy-done.1, f32[3,2,32,128]{3,2,1,0:T(8,128)S(1)} %collective-permute-done.xa_ref, f32[3,2,32,128]{3,2,1,0:T(8,128)S(1)} %collective-permute-done.1.xb_ref, ...), custom_call_target="tpu_custom_call" | custom-call | tf_op jit(solution)/shard_map/stencil/pallas_call | solution.py:235
  32.6 3.8 %collective-permute-start.4 = (f32[2,3,32,128]{3,2,1,0:T(8,128)S(1)}, f32[2,3,32,128]{3,2,1,0:T(8,128)S(1)}, u32[]{:S(2)}, u32[]{:S(2)}) collective-permute-start(f32[2,3,32,128]{3,2,1,0:T(8,128)S(1)} %get-tuple-element.14.own_ref), channel_id=1, source_target_pairs={{0,16},{16,0},{32,48},{48,32},{64,80},{80,64},{96,112},{112,96},{1... | collective-permute-start | bytes 294920 | tf_op jit(solution)/shard_map/ppermute | solution.py:250
  36.4 0.9 %collective-permute-done.4.other_ref = f32[2,3,32,128]{3,2,1,0:T(8,128)S(1)} collective-permute-done((f32[2,3,32,128]{3,2,1,0:T(8,128)S(1)}, f32[2,3,32,128]{3,2,1,0:T(8,128)S(1)}, u32[]{:S(2)}, u32[]{:S(2)}) %collective-permute-start.4) | collective-permute-done | bytes 98336 | tf_op jit(solution)/shard_map/ppermute | solution.py:250
  37.4 10.3 %all_to_all.5.all_ref = f32[8,2,3,16,128]{4,3,2,1,0:T(8,128)S(1)} all-to-all(f32[8,2,3,16,128]{4,3,2,1,0:T(8,128)S(1)} %chip.1), channel_id=1, replica_groups={{0,32,64,96,128,160,192,224},{16,48,80,112,144,176,208,240},{1,33,65,97..., dimensions={0} | all-to-all | bytes 786432 | tf_op jit(solution)/shard_map/all_to_all | solution.py:261
  47.7 1.6 %collective-permute-start.5 = (f32[2,3,16,128]{3,2,1,0:T(8,128)S(1)}, f32[2,3,16,128]{3,2,1,0:T(8,128)S(1)}, u32[]{:S(2)}, u32[]{:S(2)}) collective-permute-start(f32[2,3,16,128]{3,2,1,0:T(8,128)S(1)} %join.1.in_own_ref), channel_id=1, source_target_pairs={{0,16},{16,0},{32,48},{48,32},{64,80},{80,64},{96,112},{112,96},{1... | collective-permute-start | bytes 147464 | tf_op jit(solution)/shard_map/ppermute | solution.py:270
  49.4 0.9 %collective-permute-done.5.in_other_ref = f32[2,3,16,128]{3,2,1,0:T(8,128)S(1)} collective-permute-done((f32[2,3,16,128]{3,2,1,0:T(8,128)S(1)}, f32[2,3,16,128]{3,2,1,0:T(8,128)S(1)}, u32[]{:S(2)}, u32[]{:S(2)}) %collective-permute-start.5) | collective-permute-done | bytes 49184 | tf_op jit(solution)/shard_map/ppermute | solution.py:270
  50.3 2.4 %final.1 = f32[3,64,32,128]{3,2,1,0:T(8,128)} custom-call(f32[3,64,32,128]{3,2,1,0:T(8,128)S(1)} %get-tuple-element.13.u_ref, f32[2,3,16,128]{3,2,1,0:T(8,128)S(1)} %join.1.in_own_ref, f32[2,3,16,128]{3,2,1,0:T(8,128)S(1)} %collective-permute-done.5.in_other_ref, f32[2,3,32,128]{3,2,1,0:T(8,128)S(1)} %collective-permute-done.4.other_ref), custom_call_target="tpu_custom_call" | custom-call | tf_op jit(solution)/shard_map/final/pallas_call | solution.py:271
  (2 shorter events, 0.1 us)
Async XLA Ops:
  0.6 1.9 %copy-start = (f32[3,64,32,128]{3,2,1,0:T(8,128)S(1)}, f32[3,64,32,128]{3,2,1,0:T(8,128)}, u32[]{:S(2)}) copy-start(f32[3,64,32,128]{3,2,1,0:T(8,128)} %v_ref.3) | copy-start | bytes 9437188
  2.5 15.0 %copy-start.1 = (f32[3,64,32,128]{3,2,1,0:T(8,128)S(1)}, f32[3,64,32,128]{3,2,1,0:T(8,128)}, u32[]{:S(2)}) copy-start(f32[3,64,32,128]{3,2,1,0:T(8,128)} %v_ref.3) | copy-start | bytes 9437188
  4.5 13.0 %collective-permute-start = (f32[3,2,32,128]{3,2,1,0:T(8,128)S(1)}, f32[3,2,32,128]{3,2,1,0:T(8,128)S(1)}, u32[]{:S(2)}, u32[]{:S(2)}) collective-permute-start(f32[3,2,32,128]{3,2,1,0:T(8,128)S(1)} %get-tuple-element.9), channel_id=1, source_target_pairs={{0,16},{16,0},{32,48},{48,32},{64,80},{80,64},{96,112},{112,96},{1... | collective-permute-start | bytes 294920 | tf_op jit(solution)/shard_map/ppermute | solution.py:234
  7.9 9.7 %collective-permute-start.1 = (f32[3,2,32,128]{3,2,1,0:T(8,128)S(1)}, f32[3,2,32,128]{3,2,1,0:T(8,128)S(1)}, u32[]{:S(2)}, u32[]{:S(2)}) collective-permute-start(f32[3,2,32,128]{3,2,1,0:T(8,128)S(1)} %get-tuple-element.10), channel_id=1, source_target_pairs={{0,240},{16,32},{32,16},{48,64},{64,48},{80,96},{96,80},{112,128},... | collective-permute-start | bytes 294920 | tf_op jit(solution)/shard_map/ppermute | solution.py:233
  7.9 8.2 %collective-permute-start.2 = (f32[3,32,128]{2,1,0:T(8,128)S(1)}, f32[3,32,128]{2,1,0:T(8,128)S(1)}, u32[]{:S(2)}, u32[]{:S(2)}) collective-permute-start(f32[3,32,128]{2,1,0:T(8,128)S(1)} %get-tuple-element.11.za_ref), channel_id=1, source_target_pairs={{0,1},{1,0},{2,3},{3,2},{4,5},{5,4},{6,7},{7,6},{8,9},{9,8},{10,11... | collective-permute-start | bytes 147464 | tf_op jit(solution)/shard_map/ppermute | solution.py:232
  9.1 8.5 %collective-permute-start.3 = (f32[3,32,128]{2,1,0:T(8,128)S(1)}, f32[3,32,128]{2,1,0:T(8,128)S(1)}, u32[]{:S(2)}, u32[]{:S(2)}) collective-permute-start(f32[3,32,128]{2,1,0:T(8,128)S(1)} %get-tuple-element.12.zb_ref), channel_id=1, source_target_pairs={{0,15},{1,2},{2,1},{3,4},{4,3},{5,6},{6,5},{7,8},{8,7},{9,10},{10,... | collective-permute-start | bytes 147464 | tf_op jit(solution)/shard_map/ppermute | solution.py:231
  32.6 4.8 %collective-permute-start.4 = (f32[2,3,32,128]{3,2,1,0:T(8,128)S(1)}, f32[2,3,32,128]{3,2,1,0:T(8,128)S(1)}, u32[]{:S(2)}, u32[]{:S(2)}) collective-permute-start(f32[2,3,32,128]{3,2,1,0:T(8,128)S(1)} %get-tuple-element.14.own_ref), channel_id=1, source_target_pairs={{0,16},{16,0},{32,48},{48,32},{64,80},{80,64},{96,112},{112,96},{1... | collective-permute-start | bytes 294920 | tf_op jit(solution)/shard_map/ppermute | solution.py:250
  47.7 2.5 %collective-permute-start.5 = (f32[2,3,16,128]{3,2,1,0:T(8,128)S(1)}, f32[2,3,16,128]{3,2,1,0:T(8,128)S(1)}, u32[]{:S(2)}, u32[]{:S(2)}) collective-permute-start(f32[2,3,16,128]{3,2,1,0:T(8,128)S(1)} %join.1.in_own_ref), channel_id=1, source_target_pairs={{0,16},{16,0},{32,48},{48,32},{64,80},{80,64},{96,112},{112,96},{1... | collective-permute-start | bytes 147464 | tf_op jit(solution)/shard_map/ppermute | solution.py:270

commit v2 on v1

v2 whole, which is shorter than its diff:
```python
import math

import jax
import jax.numpy as jnp
from jax import lax
from jax.experimental import pallas as pl
from jax.experimental.pallas import tpu as pltpu
from jax.sharding import PartitionSpec as P

VISC = 12288
COURANT = 0.1

HALF = 1.0 / (2.0 * VISC)
LAM = 1.0 + HALF - math.sqrt(2.0 * HALF + HALF * HALF)
GAIN = 1.0 / (1.0 + 2.0 * VISC * (1.0 - LAM))

X = 64
Y = 32
Z = 128
CHUNK = 8
CHUNKS = X // CHUNK
GROUP = 10
LOAD = 16
LOADS = X // LOAD
GROUPS = (X - 4) // GROUP
PAD = 8
WIDE = Y + 2 * PAD
CHIPS = 8
PERIOD = 2 * X * CHIPS
F32 = jnp.float32
BF16 = jnp.bfloat16
VM = pl.BlockSpec(memory_space=pltpu.VMEM)
ANY = pl.BlockSpec(memory_space=pl.ANY)
HBM = pl.BlockSpec(memory_space=pltpu.HBM)


COST = pl.CostEstimate(flops=20_000_000, bytes_accessed=12_000_000, transcendentals=0)


def params(mib):
    return pltpu.CompilerParams(vmem_limit_bytes=mib * 1024 * 1024)


def shape(*dims):
    return jax.ShapeDtypeStruct(dims, F32)


def lanes(rows):
    return lax.broadcasted_iota(jnp.int32, (rows, Z), 1)


def shift(a, amount):
    return pltpu.roll(a, amount % Z, 1)


def split(a):
    high = a.astype(BF16)
    rest = a - high.astype(F32)
    middle = rest.astype(BF16)
    return high, middle, (rest - middle.astype(F32)).astype(BF16)


def band_matrices():
    gap = (lax.broadcasted_iota(jnp.int32, (Z, Z), 0) - lax.broadcasted_iota(jnp.int32, (Z, Z), 1)) & (Z - 1)
    band = jnp.where(gap == 1, 8.0, 0.0) - jnp.where(gap == Z - 1, 8.0, 0.0)
    band = band - jnp.where(gap == 2, 1.0, 0.0) + jnp.where(gap == Z - 2, 1.0, 0.0)
    band = band.astype(BF16)
    return band, jnp.concatenate([band, band], axis=0)


def z_by_matrix(f, bands):
    one, two, three = split(f)
    pair = jnp.concatenate([one, two], axis=1)
    total = jnp.dot(pair, bands[1], preferred_element_type=F32)
    return total + jnp.dot(three, bands[0], preferred_element_type=F32)


def z_by_shift(f):
    return 8.0 * (shift(f, -1) - shift(f, 1)) - (shift(f, -2) - shift(f, 2))


def advection(vp_ref, x, layer, bands):
    f = layer(x)
    gx = 8.0 * (layer(x + 1) - layer(x - 1)) - (layer(x + 2) - layer(x - 2))
    near = vp_ref[:, x, PAD + 1 : PAD + Y + 1] - vp_ref[:, x, PAD - 1 : PAD + Y - 1]
    gy = 8.0 * near - (vp_ref[:, x, PAD + 2 : PAD + Y + 2] - vp_ref[:, x, PAD - 2 : PAD + Y - 2])
    gz = jnp.concatenate([z_by_matrix(f[:2].reshape(2 * Y, Z), bands), z_by_shift(f[2])], axis=0)
    u = f * (1.0 / 12.0)
    return u[0][None] * gx + u[1][None] * gy + u[2][None] * gz.reshape(3, Y, Z)


def interior(vp_ref, part_ref):
    bands = band_matrices()

    def layer(x):
        return vp_ref[:, x, PAD : PAD + Y]

    def group(g, carry):
        for k in range(GROUP):
            x = 2 + g * GROUP + k
            part_ref[:, x] = advection(vp_ref, x, layer, bands)
        return carry

    lax.fori_loop(0, GROUPS, group, 0)


def place():
    return lax.rem(lax.axis_index("gz"), 8)


def pack_kernel(v_ref, zb_ref, za_ref, xb_ref, xa_ref, vp_ref, part_ref, sem):
    def v_copy(j):
        rows = pl.ds(j * LOAD, LOAD)
        return pltpu.make_async_copy(v_ref.at[:, rows], vp_ref.at[:, rows, pl.ds(PAD, Y)], sem.at[j])

    for j in range(LOADS):
        v_copy(j).start()
    slot = lanes(3 * Y) >> 1

    def chunk(j, carry):
        bottom, top = carry
        v_copy(j).wait()
        for k in range(LOAD):
            x = j * LOAD + k
            f = vp_ref[:, x, PAD : PAD + Y]
            vp_ref[:, x, PAD - 2 : PAD] = f[:, Y - 2 :]
            vp_ref[:, x, PAD + Y : PAD + Y + 2] = f[:, :2]
            turned = pltpu.roll(f.reshape(3 * Y, Z), 2 * x, 1)
            bottom = jnp.where(slot == x, turned, bottom)
            top = jnp.where(slot == lax.rem(x + X - 1, X), turned, top)
        return bottom, top

    zero = jnp.zeros((3 * Y, Z), F32)
    bottom, top = lax.fori_loop(0, LOADS, chunk, (zero, zero))
    even = lax.rem(lax.axis_index("gz"), 2) == 0
    za_ref[: 3 * Y] = jnp.where(even, top, bottom)
    zb_ref[: 3 * Y] = jnp.where(even, bottom, top)
    za_ref[3 * Y :] = jnp.zeros((za_ref.shape[0] - 3 * Y, Z), F32)
    zb_ref[3 * Y :] = jnp.zeros((zb_ref.shape[0] - 3 * Y, Z), F32)
    first = (1 - lax.rem(lax.axis_index("gx"), 2)) * (X - 2)
    xa_ref[...] = vp_ref[:, pl.ds(first, 2), PAD : PAD + Y]
    xb_ref[...] = vp_ref[:, pl.ds(X - 2 - first, 2), PAD : PAD + Y]

    @pl.when(place() == 0)
    def _():
        interior(vp_ref, part_ref)


def second_kernel(vp_ref, part_ref, za_ref, out_ref, za_out_ref):
    za_out_ref[...] = za_ref[...]

    @pl.when(place() == 1)
    def _():
        interior(vp_ref, out_ref)


def third_kernel(vp_ref, part_ref, out_ref):
    @pl.when(place() > 1)
    def _():
        interior(vp_ref, out_ref)


def stencil_kernel(
    vp_ref, part_ref, xb_ref, xa_ref, za_ref, zb_ref, rb_ref, ra_ref,
    n_ref, w_ref, r_ref, mom_ref,
    nb, edge, xlow, xhigh, nsem,
):
    x_even = lax.rem(lax.axis_index("gx"), 2) == 0
    z_even = lax.rem(lax.axis_index("gz"), 2) == 0
    xlow[...] = jnp.where(x_even, xb_ref[...], xa_ref[...])
    xhigh[...] = jnp.where(x_even, xa_ref[...], xb_ref[...])

    lane = lanes(3 * Y)
    even_lane = lane & 1 == 0
    columns = slice(0, 3 * Y)
    own_top = jnp.where(z_even, za_ref[columns], zb_ref[columns])
    own_bottom = jnp.where(z_even, zb_ref[columns], za_ref[columns])
    high = jnp.where(z_even, ra_ref[columns], rb_ref[columns]) - own_bottom
    low = jnp.where(z_even, rb_ref[columns], ra_ref[columns]) - own_top
    low_two = shift(low, 2)
    at_bottom = jnp.where(even_lane, low_two - 8.0 * shift(low, 1), low_two)
    high_two = shift(high, -2)
    at_top = jnp.where(even_lane, -high_two, 8.0 * shift(high, -1) - high_two)
    early = lane & 3 < 2
    edge[0] = jnp.where(early, at_bottom, at_top)
    edge[1] = jnp.where(early, at_top, at_bottom)
    border = (lane < 2) | (lane >= Z - 2)

    bands = band_matrices()

    def layer(x):
        if isinstance(x, int) and x < 0:
            return xlow[:, x + 2]
        if isinstance(x, int) and x >= X:
            return xhigh[:, x - X]
        return vp_ref[:, x, PAD : PAD + Y]

    def row(x, odd, p, q, power, part):
        f = layer(x)
        fix = jnp.where(border, pltpu.roll(edge[odd], lax.rem(2 * (X - x), Z), 1), 0.0)
        n = part + (f[2] * (1.0 / 12.0))[None] * fix.reshape(3, Y, Z)
        w = (2.0 * GAIN) * f - (COURANT * GAIN) * n
        p = LAM * p + w
        q = q + power * w
        nb[:, x] = n
        w_ref[:, x] = w
        r_ref[:, x] = p - f
        return p, q

    def n_copy(start, size, k):
        rows = pl.ds(start, size)
        return pltpu.make_async_copy(nb.at[:, rows], n_ref.at[:, rows], nsem.at[k])

    p = jnp.zeros((3, Y, Z), F32)
    q = p
    for x in (0, 1):
        p, q = row(x, x % 2, p, q, LAM**x, advection(vp_ref, x, layer, bands))
    n_copy(0, 2, GROUPS).start()

    def group(g, carry):
        p, q, power = carry
        for k in range(GROUP):
            x = 2 + g * GROUP + k
            p, q = row(x, k % 2, p, q, power, part_ref[:, x])
            power = power * LAM
        n_copy(2 + g * GROUP, GROUP, g).start()
        return p, q, power

    p, q, _ = lax.fori_loop(0, GROUPS, group, (p, q, F32(LAM**2)))
    for x in (X - 2, X - 1):
        p, q = row(x, x % 2, p, q, LAM**x, advection(vp_ref, x, layer, bands))
    n_copy(X - 2, 2, GROUPS + 1).start()
    mom_ref[0] = p
    mom_ref[1] = q
    n_copy(0, 2, GROUPS).wait()
    for g in range(GROUPS):
        n_copy(2 + g * GROUP, GROUP, g).wait()
    n_copy(X - 2, 2, GROUPS + 1).wait()


def chip_kernel(own_ref, other_ref, out_ref):
    core = lax.rem(lax.axis_index("gx"), 2)
    rows = pl.ds(pl.multiple_of(core * (Y // 2), Y // 2), Y // 2)
    own_p, own_q = own_ref[0, :, rows], own_ref[1, :, rows]
    other_p, other_q = other_ref[0, :, rows], other_ref[1, :, rows]
    first = core == 0
    far = LAM**X
    p = jnp.where(first, own_p, other_p) * far + jnp.where(first, other_p, own_p)
    q = jnp.where(first, own_q, other_q) + far * jnp.where(first, other_q, own_q)
    for k in range(CHIPS):
        out_ref[k, 0] = p
        out_ref[k, 1] = q


def join_kernel(all_ref, out_ref):
    chip = lax.div(lax.axis_index("gx"), 2)
    p = jnp.zeros(all_ref.shape[2:], F32)
    q = p
    for s in range(1, CHIPS + 1):
        weight = LAM ** (2 * X * (s - 1)) / (1.0 - LAM**PERIOD)
        p = p + weight * all_ref[lax.rem(chip + CHIPS - s % CHIPS, CHIPS), 0]
        q = q + weight * all_ref[lax.rem(chip + s, CHIPS), 1]
    out_ref[0] = p
    out_ref[1] = q


def final_kernel(w_ref, r_ref, in_own_ref, in_other_ref, other_ref, out_ref, ob, osem):
    def o_copy(j):
        rows = pl.ds(j * CHUNK, CHUNK)
        return pltpu.make_async_copy(ob.at[:, rows], out_ref.at[:, rows], osem.at[j])

    first = lax.rem(lax.axis_index("gx"), 2) == 0
    own, other = in_own_ref[...], in_other_ref[...]
    both = jnp.concatenate([jnp.where(first, own, other), jnp.where(first, other, own)], axis=2)
    far = LAM**X
    p_in = jnp.where(first, both[0], other_ref[0] + far * both[0])
    q_in = jnp.where(first, other_ref[1] + far * both[1], both[1])

    def chunk(i, carry):
        p, q = carry
        j = CHUNKS - 1 - i
        for k in reversed(range(CHUNK)):
            x = j * CHUNK + k
            q = LAM * q
            ob[:, x] = (r_ref[:, x] + p) + q
            q = q + w_ref[:, x]
            p = p * (1.0 / LAM)
        o_copy(j).start()
        return p, q

    lax.fori_loop(0, CHUNKS, chunk, (far * p_in, q_in))
    for j in range(CHUNKS):
        o_copy(j).wait()


def pair_low(count):
    return [(i, i ^ 1) for i in range(count)]


def pair_high(count):
    return [(i, (i + 1 if i % 2 else i - 1) % count) for i in range(count)]


def shards(v):
    nx, nz = lax.axis_size("gx"), lax.axis_size("gz")
    v = pltpu.with_memory_space_constraint(v, pltpu.HBM)
    sems = [pltpu.SemaphoreType.DMA((CHUNKS,))]
    part_shape = pltpu.VMEM((3, X, Y, Z), F32)
    zb, za, xb, xa, vp, part = pl.pallas_call(
        pack_kernel,
        out_shape=[shape(208, Z), shape(200, Z)] + [shape(3, 2, Y, Z)] * 2 + [shape(3, X, WIDE, Z), part_shape],
        in_specs=[HBM],
        out_specs=[VM] * 6,
        scratch_shapes=[pltpu.SemaphoreType.DMA((LOADS,))],
        compiler_params=params(16),
        name="pack",
    )(v)
    rzb = lax.ppermute(zb, "gz", pair_high(nz))
    part, za = pl.pallas_call(
        second_kernel,
        out_shape=[part_shape, shape(200, Z)],
        in_specs=[VM] * 3,
        out_specs=[VM] * 2,
        input_output_aliases={1: 0},
        compiler_params=params(16),
        cost_estimate=COST,
        name="second",
    )(vp, part, za)
    rza = lax.ppermute(za, "gz", pair_low(nz))
    rxb = lax.ppermute(xb, "gx", pair_high(nx))
    rxa = lax.ppermute(xa, "gx", pair_low(nx))
    part = pl.pallas_call(
        third_kernel,
        out_shape=part_shape,
        in_specs=[VM] * 2,
        out_specs=VM,
        input_output_aliases={1: 0},
        compiler_params=params(16),
        cost_estimate=COST,
        name="third",
    )(vp, part)
    n, w, r, mom = pl.pallas_call(
        stencil_kernel,
        out_shape=[shape(3, X, Y, Z)] * 3 + [shape(2, 3, Y, Z)],
        in_specs=[VM] * 8,
        out_specs=[ANY, VM, VM, VM],
        scratch_shapes=[
            pltpu.VMEM((3, X, Y, Z), F32),
            pltpu.VMEM((2, 3 * Y, Z), F32),
            pltpu.VMEM((3, 2, Y, Z), F32),
            pltpu.VMEM((3, 2, Y, Z), F32),
            pltpu.SemaphoreType.DMA((GROUPS + 2,)),
        ],
        compiler_params=params(24),
        name="stencil",
    )(vp, part, rxb, rxa, za, zb, rzb, rza)
    other = lax.ppermute(mom, "gx", pair_low(nx))
    half = (2, 3, Y // 2, Z)
    chip = pl.pallas_call(
        chip_kernel,
        out_shape=shape(CHIPS, *half),
        in_specs=[VM, VM],
        out_specs=VM,
        compiler_params=params(16),
        name="chip",
    )(mom, other)
    groups = [[core + 2 * k for k in range(CHIPS)] for core in range(2)]
    everyone = lax.all_to_all(chip, "gx", 0, 0, axis_index_groups=groups)
    joined = pl.pallas_call(
        join_kernel,
        out_shape=shape(*half),
        in_specs=[VM],
        out_specs=VM,
        compiler_params=params(16),
        name="join",
    )(everyone)
    joined_other = lax.ppermute(joined, "gx", pair_low(nx))
    new = pl.pallas_call(
        final_kernel,
        out_shape=shape(3, X, Y, Z),
        in_specs=[VM] * 5,
        out_specs=ANY,
        scratch_shapes=[pltpu.VMEM((3, X, Y, Z), F32)] + sems,
        compiler_params=params(16),
        name="final",
    )(w, r, joined, joined_other, other)
    return new, n


def solution(mesh):
    spec = P(None, "gx", None, "gz")
    return jax.shard_map(shards, mesh=mesh, in_specs=(spec,), out_specs=(spec, spec), check_vma=False)
```

time: 52.8 us -> 39.7 us (0.75)
  Pallas kernels: 19.5 us -> 10.5 us
  starting transfers between devices: 17 us -> 12.9 us
  local copies, waits for them, and re-layouts: 1.89 us -> 0 us
  blocking collectives: 10.3 us -> 11.6 us
  waiting for transfers between devices: 3.31 us -> 3.88 us
    pallas_call x3 -> x5, Pallas kernels: 19.4 us -> 10.5 us  [the longest x1 5.77 us: shards(): pl.pallas_call(pack_kernel, out_shape=[shape(208, Z), shape(200, Z)] + [s...]
    ppermute x1, waiting for transfers between devices: 0.01 us -> 2.05 us  [shards(): rxb = lax.ppermute(xb, 'gx', pair_high(nx))]
    unnamed x4 -> x0, local copies, waits for them, and re-layouts: 1.89 us -> none
    ppermute x1, starting transfers between devices: 3.84 us -> 2.15 us  [shards(): other = lax.ppermute(mom, 'gx', pair_low(nx))]
    ppermute x1, starting transfers between devices: 3.33 us -> 1.75 us  [shards(): rxa = lax.ppermute(xa, 'gx', pair_low(nx))]
    ppermute x1, waiting for transfers between devices: 1.47 us -> 0.01 us  [shards(): rzb = lax.ppermute(zb, 'gz', pair_high(nz))]
    ppermute x1, starting transfers between devices: 7 us -> 5.68 us  [shards(): rzb = lax.ppermute(zb, 'gz', pair_high(nz))]
    ppermute x1, starting transfers between devices: 0.01 us -> 1.32 us  [shards(): rxb = lax.ppermute(xb, 'gx', pair_high(nx))]
where the time goes in v2:
time: 39.7 us; the launch traced here: 39.6 us
  starting transfers between devices  12.9 us (32%)
  blocking collectives  11.6 us (29%)
  Pallas kernels  10.5 us (26%)
  waiting for transfers between devices  3.88 us (10%)
  between operations  0.67 us (2%)
    all_to_all x1, blocking collectives, shards(): everyone = lax.all_to_all(chip, 'gx', 0, 0, axis_index_groups=groups)  11.6 us
    pallas_call x1, Pallas kernels, shards(): pl.pallas_call(pack_kernel, out_shape=[shape(208, Z), shape(200, Z)] + [s...  5.77 us
    ppermute x1, starting transfers between devices, shards(): rzb = lax.ppermute(zb, 'gz', pair_high(nz))  5.68 us
    pallas_call x1, Pallas kernels, shards(): pl.pallas_call(stencil_kernel, out_shape=[shape(3, X, Y, Z)] * 3 + [shape...  2.85 us
    ppermute x1, starting transfers between devices, shards(): other = lax.ppermute(mom, 'gx', pair_low(nx))  2.15 us
    ppermute x1, waiting for transfers between devices, shards(): rxb = lax.ppermute(xb, 'gx', pair_high(nx))  2.05 us
    ppermute x1, starting transfers between devices, shards(): joined_other = lax.ppermute(joined, 'gx', pair_low(nx))  1.95 us
    pallas_call x1, Pallas kernels, shards(): pl.pallas_call(final_kernel, out_shape=shape(3, X, Y, Z), in_specs=[VM] *...  1.82 us
  transfers between devices with their start and end apart: 6, of which 3 were waited for; matrix products, arithmetic and copies ran while one was open for 0% of the time, Pallas kernels for 0%

profile of v2, /device:TPU:1, one launch (start us, length us, event | category | flops | bytes accessed | tf_op | source)
XLA Modules:
  0.0 39.6 jit_solution(14419830104286866162)
XLA Ops:
  0.6 5.8 %pack.1 = (f32[208,128]{1,0:T(8,128)S(1)}, f32[200,128]{1,0:T(8,128)S(1)}, f32[3,2,32,128]{3,2,1,0:T(8,128)S(1)}, f32[3,2,32,128]{3,2,1,0:T(8,128)S(1)}, f32[3,6...) custom-call(f32[3,64,32,128]{3,2,1,0:T(8,128)} %v_ref.1), custom_call_target="tpu_custom_call" | custom-call | tf_op jit(solution)/shard_map/pack/pallas_call | solution.py:309
  6.4 5.7 %collective-permute-start.2 = (f32[208,128]{1,0:T(8,128)S(1)}, f32[208,128]{1,0:T(8,128)S(1)}, u32[]{:S(2)}, u32[]{:S(2)}) collective-permute-start(f32[208,128]{1,0:T(8,128)S(1)} %get-tuple-element.21.zb_ref), channel_id=1, source_target_pairs={{0,15},{1,2},{2,1},{3,4},{4,3},{5,6},{6,5},{7,8},{8,7},{9,10},{10,... | collective-permute-start | bytes 319496 | tf_op jit(solution)/shard_map/ppermute | solution.py:318
  12.1 0.1 collective-permute-start.3
  12.2 1.3 %collective-permute-start = (f32[3,2,32,128]{3,2,1,0:T(8,128)S(1)}, f32[3,2,32,128]{3,2,1,0:T(8,128)S(1)}, u32[]{:S(2)}, u32[]{:S(2)}) collective-permute-start(f32[3,2,32,128]{3,2,1,0:T(8,128)S(1)} %get-tuple-element.18), channel_id=1, source_target_pairs={{0,240},{16,32},{32,16},{48,64},{64,48},{80,96},{96,80},{112,128},... | collective-permute-start | bytes 294920 | tf_op jit(solution)/shard_map/ppermute | solution.py:330
  13.5 1.7 %collective-permute-start.1 = (f32[3,2,32,128]{3,2,1,0:T(8,128)S(1)}, f32[3,2,32,128]{3,2,1,0:T(8,128)S(1)}, u32[]{:S(2)}, u32[]{:S(2)}) collective-permute-start(f32[3,2,32,128]{3,2,1,0:T(8,128)S(1)} %get-tuple-element.19), channel_id=1, source_target_pairs={{0,16},{16,0},{32,48},{48,32},{64,80},{80,64},{96,112},{112,96},{1... | collective-permute-start | bytes 294920 | tf_op jit(solution)/shard_map/ppermute | solution.py:331
  15.3 2.0 %collective-permute-done.xb_ref = f32[3,2,32,128]{3,2,1,0:T(8,128)S(1)} collective-permute-done((f32[3,2,32,128]{3,2,1,0:T(8,128)S(1)}, f32[3,2,32,128]{3,2,1,0:T(8,128)S(1)}, u32[]{:S(2)}, u32[]{:S(2)}) %collective-permute-start) | collective-permute-done | bytes 98336 | tf_op jit(solution)/shard_map/ppermute | solution.py:330
  17.3 0.0 collective-permute-done.1.xa_ref
  17.3 0.0 collective-permute-done.3.ra_ref
  17.3 0.0 collective-permute-done.2.rb_ref
  17.3 2.9 %stencil.1 = (f32[3,64,32,128]{3,2,1,0:T(8,128)}, f32[3,64,32,128]{3,2,1,0:T(8,128)S(1)}, f32[3,64,32,128]{3,2,1,0:T(8,128)S(1)}, f32[2,3,32,128]{3,2,1,0:T(8,128)S(1)}) custom-call(f32[3,64,48,128]{3,2,1,0:T(8,128)S(1)} %get-tuple-element.14.vp_ref, f32[3,64,32,128]{3,2,1,0:T(8,128)S(1)} %third.1.part_ref, ...), custom_call_target="tpu_custom_call" | custom-call | tf_op jit(solution)/shard_map/stencil/pallas_call | solution.py:342
  20.2 2.2 %collective-permute-start.4 = (f32[2,3,32,128]{3,2,1,0:T(8,128)S(1)}, f32[2,3,32,128]{3,2,1,0:T(8,128)S(1)}, u32[]{:S(2)}, u32[]{:S(2)}) collective-permute-start(f32[2,3,32,128]{3,2,1,0:T(8,128)S(1)} %get-tuple-element.24.own_ref), channel_id=1, source_target_pairs={{0,16},{16,0},{32,48},{48,32},{64,80},{80,64},{96,112},{112,96},{1... | collective-permute-start | bytes 294920 | tf_op jit(solution)/shard_map/ppermute | solution.py:357
  22.4 0.9 %collective-permute-done.4.other_ref = f32[2,3,32,128]{3,2,1,0:T(8,128)S(1)} collective-permute-done((f32[2,3,32,128]{3,2,1,0:T(8,128)S(1)}, f32[2,3,32,128]{3,2,1,0:T(8,128)S(1)}, u32[]{:S(2)}, u32[]{:S(2)}) %collective-permute-start.4) | collective-permute-done | bytes 98336 | tf_op jit(solution)/shard_map/ppermute | solution.py:357
  23.3 11.6 %all_to_all.5.all_ref = f32[8,2,3,16,128]{4,3,2,1,0:T(8,128)S(1)} all-to-all(f32[8,2,3,16,128]{4,3,2,1,0:T(8,128)S(1)} %chip.1), channel_id=1, replica_groups={{0,32,64,96,128,160,192,224},{16,48,80,112,144,176,208,240},{1,33,65,97..., dimensions={0} | all-to-all | bytes 786432 | tf_op jit(solution)/shard_map/all_to_all | solution.py:368
  35.0 1.9 %collective-permute-start.5 = (f32[2,3,16,128]{3,2,1,0:T(8,128)S(1)}, f32[2,3,16,128]{3,2,1,0:T(8,128)S(1)}, u32[]{:S(2)}, u32[]{:S(2)}) collective-permute-start(f32[2,3,16,128]{3,2,1,0:T(8,128)S(1)} %join.1.in_own_ref), channel_id=1, source_target_pairs={{0,16},{16,0},{32,48},{48,32},{64,80},{80,64},{96,112},{112,96},{1... | collective-permute-start | bytes 147464 | tf_op jit(solution)/shard_map/ppermute | solution.py:377
  36.9 0.9 %collective-permute-done.5.in_other_ref = f32[2,3,16,128]{3,2,1,0:T(8,128)S(1)} collective-permute-done((f32[2,3,16,128]{3,2,1,0:T(8,128)S(1)}, f32[2,3,16,128]{3,2,1,0:T(8,128)S(1)}, u32[]{:S(2)}, u32[]{:S(2)}) %collective-permute-start.5) | collective-permute-done | bytes 49184 | tf_op jit(solution)/shard_map/ppermute | solution.py:377
  37.8 1.8 %final.1 = f32[3,64,32,128]{3,2,1,0:T(8,128)} custom-call(f32[3,64,32,128]{3,2,1,0:T(8,128)S(1)} %get-tuple-element.22.w_ref, f32[3,64,32,128]{3,2,1,0:T(8,128)S(1)} %get-tuple-element.23.r_ref, f32[2,3,16,128]{3,2,1,0:T(8,128)S(1)} %join.1.in_own_ref, f32[2,3,16,128]{3,2,1,0:T(8,128)S(1)} %collective-permute-done.5.in_other_ref, ...), custom_call_target="tpu_custom_call" | custom-call | tf_op jit(solution)/shard_map/final/pallas_call | solution.py:378
  (4 shorter events, 0.1 us)
Async XLA Ops:
  6.4 10.9 %collective-permute-start.2 = (f32[208,128]{1,0:T(8,128)S(1)}, f32[208,128]{1,0:T(8,128)S(1)}, u32[]{:S(2)}, u32[]{:S(2)}) collective-permute-start(f32[208,128]{1,0:T(8,128)S(1)} %get-tuple-element.21.zb_ref), channel_id=1, source_target_pairs={{0,15},{1,2},{2,1},{3,4},{4,3},{5,6},{6,5},{7,8},{8,7},{9,10},{10,... | collective-permute-start | bytes 319496 | tf_op jit(solution)/shard_map/ppermute | solution.py:318
  12.1 5.2 %collective-permute-start.3 = (f32[200,128]{1,0:T(8,128)S(1)}, f32[200,128]{1,0:T(8,128)S(1)}, u32[]{:S(2)}, u32[]{:S(2)}) collective-permute-start(f32[200,128]{1,0:T(8,128)S(1)} %get-tuple-element.20.za_ref), channel_id=1, source_target_pairs={{0,1},{1,0},{2,3},{3,2},{4,5},{5,4},{6,7},{7,6},{8,9},{9,8},{10,11... | collective-permute-start | bytes 307208 | tf_op jit(solution)/shard_map/ppermute | solution.py:329
  12.2 5.1 %collective-permute-start = (f32[3,2,32,128]{3,2,1,0:T(8,128)S(1)}, f32[3,2,32,128]{3,2,1,0:T(8,128)S(1)}, u32[]{:S(2)}, u32[]{:S(2)}) collective-permute-start(f32[3,2,32,128]{3,2,1,0:T(8,128)S(1)} %get-tuple-element.18), channel_id=1, source_target_pairs={{0,240},{16,32},{32,16},{48,64},{64,48},{80,96},{96,80},{112,128},... | collective-permute-start | bytes 294920 | tf_op jit(solution)/shard_map/ppermute | solution.py:330
  13.5 3.8 %collective-permute-start.1 = (f32[3,2,32,128]{3,2,1,0:T(8,128)S(1)}, f32[3,2,32,128]{3,2,1,0:T(8,128)S(1)}, u32[]{:S(2)}, u32[]{:S(2)}) collective-permute-start(f32[3,2,32,128]{3,2,1,0:T(8,128)S(1)} %get-tuple-element.19), channel_id=1, source_target_pairs={{0,16},{16,0},{32,48},{48,32},{64,80},{80,64},{96,112},{112,96},{1... | collective-permute-start | bytes 294920 | tf_op jit(solution)/shard_map/ppermute | solution.py:331
  20.2 3.1 %collective-permute-start.4 = (f32[2,3,32,128]{3,2,1,0:T(8,128)S(1)}, f32[2,3,32,128]{3,2,1,0:T(8,128)S(1)}, u32[]{:S(2)}, u32[]{:S(2)}) collective-permute-start(f32[2,3,32,128]{3,2,1,0:T(8,128)S(1)} %get-tuple-element.24.own_ref), channel_id=1, source_target_pairs={{0,16},{16,0},{32,48},{48,32},{64,80},{80,64},{96,112},{112,96},{1... | collective-permute-start | bytes 294920 | tf_op jit(solution)/shard_map/ppermute | solution.py:357
  35.0 2.8 %collective-permute-start.5 = (f32[2,3,16,128]{3,2,1,0:T(8,128)S(1)}, f32[2,3,16,128]{3,2,1,0:T(8,128)S(1)}, u32[]{:S(2)}, u32[]{:S(2)}) collective-permute-start(f32[2,3,16,128]{3,2,1,0:T(8,128)S(1)} %join.1.in_own_ref), channel_id=1, source_target_pairs={{0,16},{16,0},{32,48},{48,32},{64,80},{80,64},{96,112},{112,96},{1... | collective-permute-start | bytes 147464 | tf_op jit(solution)/shard_map/ppermute | solution.py:377

commit v3 on v2

--- a/solution.py
+++ b/solution.py
@@ -160,16 +160,22 @@
         interior(vp_ref, out_ref)
 
 
+def border_term(edge, x, u_z):
+    lane = lanes(3 * Y)
+    border = (lane < 2) | (lane >= Z - 2)
+    fix = jnp.where(border, pltpu.roll(edge, lax.rem(2 * (X - x), Z), 1), 0.0)
+    return u_z[None] * fix.reshape(3, Y, Z)
+
+
+def source(f, n):
+    return (2.0 * GAIN) * f - (COURANT * GAIN) * n
+
+
 def stencil_kernel(
-    vp_ref, part_ref, xb_ref, xa_ref, za_ref, zb_ref, rb_ref, ra_ref,
-    n_ref, w_ref, r_ref, mom_ref,
-    nb, edge, xlow, xhigh, nsem,
+    vp_ref, part_ref, za_ref, zb_ref, rb_ref, ra_ref,
+    n_ref, w_ref, r_ref, sum_ref, edge_ref,
 ):
-    x_even = lax.rem(lax.axis_index("gx"), 2) == 0
     z_even = lax.rem(lax.axis_index("gz"), 2) == 0
-    xlow[...] = jnp.where(x_even, xb_ref[...], xa_ref[...])
-    xhigh[...] = jnp.where(x_even, xa_ref[...], xb_ref[...])
-
     lane = lanes(3 * Y)
     even_lane = lane & 1 == 0
     columns = slice(0, 3 * Y)
@@ -182,63 +188,87 @@
     high_two = shift(high, -2)
     at_top = jnp.where(even_lane, -high_two, 8.0 * shift(high, -1) - high_two)
     early = lane & 3 < 2
-    edge[0] = jnp.where(early, at_bottom, at_top)
-    edge[1] = jnp.where(early, at_top, at_bottom)
-    border = (lane < 2) | (lane >= Z - 2)
-
-    bands = band_matrices()
-
-    def layer(x):
-        if isinstance(x, int) and x < 0:
-            return xlow[:, x + 2]
-        if isinstance(x, int) and x >= X:
-            return xhigh[:, x - X]
-        return vp_ref[:, x, PAD : PAD + Y]
-
-    def row(x, odd, p, q, power, part):
-        f = layer(x)
-        fix = jnp.where(border, pltpu.roll(edge[odd], lax.rem(2 * (X - x), Z), 1), 0.0)
-        n = part + (f[2] * (1.0 / 12.0))[None] * fix.reshape(3, Y, Z)
-        w = (2.0 * GAIN) * f - (COURANT * GAIN) * n
-        p = LAM * p + w
-        q = q + power * w
-        nb[:, x] = n
-        w_ref[:, x] = w
-        r_ref[:, x] = p - f
-        return p, q
-
-    def n_copy(start, size, k):
-        rows = pl.ds(start, size)
-        return pltpu.make_async_copy(nb.at[:, rows], n_ref.at[:, rows], nsem.at[k])
-
-    p = jnp.zeros((3, Y, Z), F32)
-    q = p
-    for x in (0, 1):
-        p, q = row(x, x % 2, p, q, LAM**x, advection(vp_ref, x, layer, bands))
-    n_copy(0, 2, GROUPS).start()
+    edge_ref[0] = jnp.where(early, at_bottom, at_top)
+    edge_ref[1] = jnp.where(early, at_top, at_bottom)
 
     def group(g, carry):
         p, q, power = carry
         for k in range(GROUP):
             x = 2 + g * GROUP + k
-            p, q = row(x, k % 2, p, q, power, part_ref[:, x])
+            f = vp_ref[:, x, PAD : PAD + Y]
+            n = part_ref[:, x] + border_term(edge_ref[k % 2], x, f[2] * (1.0 / 12.0))
+            w = source(f, n)
+            p = LAM * p + w
+            q = q + power * w
+            n_ref[:, x] = n
+            w_ref[:, x] = w
+            r_ref[:, x] = p - f
             power = power * LAM
-        n_copy(2 + g * GROUP, GROUP, g).start()
         return p, q, power
 
-    p, q, _ = lax.fori_loop(0, GROUPS, group, (p, q, F32(LAM**2)))
-    for x in (X - 2, X - 1):
-        p, q = row(x, x % 2, p, q, LAM**x, advection(vp_ref, x, layer, bands))
-    n_copy(X - 2, 2, GROUPS + 1).start()
-    mom_ref[0] = p
-    mom_ref[1] = q
-    n_copy(0, 2, GROUPS).wait()
-    for g in range(GROUPS):
-        n_copy(2 + g * GROUP, GROUP, g).wait()
-    n_copy(X - 2, 2, GROUPS + 1).wait()
-
-
-def chip_kernel(own_ref, other_ref, out_ref):
+    zero = jnp.zeros((3, Y, Z), F32)
+    sum_ref[0], sum_ref[1], _ = lax.fori_loop(0, GROUPS, group, (zero, zero, F32(1.0)))
+
+
+def ends_kernel(
+    vp_ref, edge_ref, sum_ref, xb_ref, xa_ref,
+    n_ref, w_ref, r_ref, start_ref, mom_ref,
+):
+    x_even = lax.rem(lax.axis_index("gx"), 2) == 0
+    xlow = jnp.where(x_even, xb_ref[...], xa_ref[...])
+    xhigh = jnp.where(x_even, xa_ref[...], xb_ref[...])
+    bands = band_matrices()
+
+    def layer(x):
+        if x < 0:
+            return xlow[:, x + 2]
+        if x >= X:
+            return xhigh[:, x - X]
+        return vp_ref[:, x, PAD : PAD + Y]
+
+    fields, sources = [], []
+    for k, x in enumerate((0, 1, X - 2, X - 1)):
+        f = layer(x)
+        n = advection(vp_ref, x, layer, bands) + border_term(edge_ref[x % 2], x, f[2] * (1.0 / 12.0))
+        w = source(f, n)
+        n_ref[:, k] = n
+        w_ref[:, k] = w
+        fields.append(f)
+        sources.append(w)
+    start = LAM * sources[0] + sources[1]
+    before_last = LAM * (sum_ref[0] + LAM ** (X - 4) * start) + sources[2]
+    last = LAM * before_last + sources[3]
+    for k, p in enumerate((sources[0], start, before_last, last)):
+        r_ref[:, k] = p - fields[k]
+    start_ref[...] = start
+    mom_ref[0] = last
+    ends = LAM ** (X - 2) * sources[2] + LAM ** (X - 1) * sources[3]
+    mom_ref[1] = sources[0] + LAM * sources[1] + LAM**2 * sum_ref[1] + ends
+
+
+def store_first_kernel(n_ref, ends_ref, out_ref, sems):
+    copies = [
+        pltpu.make_async_copy(n_ref.at[:, 2 : X // 2], out_ref.at[:, 2 : X // 2], sems.at[0]),
+        pltpu.make_async_copy(ends_ref.at[:, 0:2], out_ref.at[:, 0:2], sems.at[1]),
+    ]
+    for copy in copies:
+        copy.start()
+    for copy in copies:
+        copy.wait()
+
+
+def store_last_kernel(n_ref, ends_ref, started_ref, out_ref, sems):
+    copies = [
+        pltpu.make_async_copy(n_ref.at[:, X // 2 : X - 2], out_ref.at[:, X // 2 : X - 2], sems.at[0]),
+        pltpu.make_async_copy(ends_ref.at[:, 2:4], out_ref.at[:, X - 2 : X], sems.at[1]),
+    ]
+    for copy in copies:
+        copy.start()
+    for copy in copies:
+        copy.wait()
+
+
+def chip_kernel(own_ref, other_ref, started_ref, out_ref):
     core = lax.rem(lax.axis_index("gx"), 2)
     rows = pl.ds(pl.multiple_of(core * (Y // 2), Y // 2), Y // 2)
     own_p, own_q = own_ref[0, :, rows], own_ref[1, :, rows]
@@ -264,33 +294,49 @@
     out_ref[1] = q
 
 
-def final_kernel(w_ref, r_ref, in_own_ref, in_other_ref, other_ref, out_ref, ob, osem):
-    def o_copy(j):
-        rows = pl.ds(j * CHUNK, CHUNK)
-        return pltpu.make_async_copy(ob.at[:, rows], out_ref.at[:, rows], osem.at[j])
+def final_kernel(
+    w_ref, r_ref, wend_ref, rend_ref, start_ref, in_own_ref, in_other_ref, other_ref, out_ref, ob, osem,
+):
+    def o_copy(start, size, k):
+        rows = pl.ds(start, size)
+        return pltpu.make_async_copy(ob.at[:, rows], out_ref.at[:, rows], osem.at[k])
 
     first = lax.rem(lax.axis_index("gx"), 2) == 0
     own, other = in_own_ref[...], in_other_ref[...]
     both = jnp.concatenate([jnp.where(first, own, other), jnp.where(first, other, own)], axis=2)
     far = LAM**X
     p_in = jnp.where(first, both[0], other_ref[0] + far * both[0])
-    q_in = jnp.where(first, other_ref[1] + far * both[1], both[1])
-
-    def chunk(i, carry):
+    q = jnp.where(first, other_ref[1] + far * both[1], both[1])
+
+    for k, x in ((3, X - 1), (2, X - 2)):
+        q = LAM * q
+        ob[:, x] = (rend_ref[:, k] + LAM ** (x + 1) * p_in) + q
+        q = q + wend_ref[:, k]
+    o_copy(X - 2, 2, GROUPS).start()
+
+    def group(i, carry):
         p, q = carry
-        j = CHUNKS - 1 - i
-        for k in reversed(range(CHUNK)):
-            x = j * CHUNK + k
+        g = GROUPS - 1 - i
+        for k in reversed(range(GROUP)):
+            x = 2 + g * GROUP + k
             q = LAM * q
             ob[:, x] = (r_ref[:, x] + p) + q
             q = q + w_ref[:, x]
             p = p * (1.0 / LAM)
-        o_copy(j).start()
+        o_copy(2 + g * GROUP, GROUP, g).start()
         return p, q
 
-    lax.fori_loop(0, CHUNKS, chunk, (far * p_in, q_in))
-    for j in range(CHUNKS):
-        o_copy(j).wait()
+    p = LAM ** (X - 2) * p_in + LAM ** (X - 4) * start_ref[...]
+    _, q = lax.fori_loop(0, GROUPS, group, (p, q))
+    for x in (1, 0):
+        q = LAM * q
+        ob[:, x] = (rend_ref[:, x] + LAM ** (x + 1) * p_in) + q
+        q = q + wend_ref[:, x]
+    o_copy(0, 2, GROUPS + 1).start()
+    o_copy(X - 2, 2, GROUPS).wait()
+    for g in range(GROUPS):
+        o_copy(2 + g * GROUP, GROUP, g).wait()
+    o_copy(0, 2, GROUPS + 1).wait()
 
 
 def pair_low(count):
@@ -339,31 +385,45 @@
         cost_estimate=COST,
         name="third",
     )(vp, part)
-    n, w, r, mom = pl.pallas_call(
+    n, w, r, sums, edge = pl.pallas_call(
         stencil_kernel,
-        out_shape=[shape(3, X, Y, Z)] * 3 + [shape(2, 3, Y, Z)],
-        in_specs=[VM] * 8,
-        out_specs=[ANY, VM, VM, VM],
-        scratch_shapes=[
-            pltpu.VMEM((3, X, Y, Z), F32),
-            pltpu.VMEM((2, 3 * Y, Z), F32),
-            pltpu.VMEM((3, 2, Y, Z), F32),
-            pltpu.VMEM((3, 2, Y, Z), F32),
-            pltpu.SemaphoreType.DMA((GROUPS + 2,)),
-        ],
-        compiler_params=params(24),
+        out_shape=[part_shape] * 3 + [shape(2, 3, Y, Z), shape(2, 3 * Y, Z)],
+        in_specs=[VM] * 6,
+        out_specs=[VM] * 5,
+        compiler_params=params(16),
+        cost_estimate=COST,
         name="stencil",
-    )(vp, part, rxb, rxa, za, zb, rzb, rza)
+    )(vp, part, za, zb, rzb, rza)
+    n_ends, w_ends, r_ends, start, mom = pl.pallas_call(
+        ends_kernel,
+        out_shape=[shape(3, 4, Y, Z)] * 3 + [shape(3, Y, Z), shape(2, 3, Y, Z)],
+        in_specs=[VM] * 5,
+        out_specs=[VM] * 5,
+        compiler_params=params(16),
+        name="ends",
+    )(vp, edge, sums, rxb, rxa)
     other = lax.ppermute(mom, "gx", pair_low(nx))
+    half_cost = pl.CostEstimate(flops=0, bytes_accessed=4_000_000, transcendentals=0)
+    stored = pl.pallas_call(
+        store_first_kernel,
+        out_shape=shape(3, X, Y, Z),
+        in_specs=[VM] * 2,
+        out_specs=HBM,
+        scratch_shapes=[pltpu.SemaphoreType.DMA((2,))],
+        compiler_params=params(8),
+        cost_estimate=half_cost,
+        name="store_first",
+    )(n, n_ends)
+    stored = pltpu.with_memory_space_constraint(stored, pltpu.HBM)
     half = (2, 3, Y // 2, Z)
     chip = pl.pallas_call(
         chip_kernel,
         out_shape=shape(CHIPS, *half),
-        in_specs=[VM, VM],
+        in_specs=[VM, VM, HBM],
         out_specs=VM,
         compiler_params=params(16),
         name="chip",
-    )(mom, other)
+    )(mom, other, stored)
     groups = [[core + 2 * k for k in range(CHIPS)] for core in range(2)]
     everyone = lax.all_to_all(chip, "gx", 0, 0, axis_index_groups=groups)
     joined = pl.pallas_call(
@@ -375,16 +435,27 @@
         name="join",
     )(everyone)
     joined_other = lax.ppermute(joined, "gx", pair_low(nx))
+    stored = pl.pallas_call(
+        store_last_kernel,
+        out_shape=shape(3, X, Y, Z),
+        in_specs=[VM, VM, HBM],
+        out_specs=HBM,
+        input_output_aliases={2: 0},
+        scratch_shapes=[pltpu.SemaphoreType.DMA((2,))],
+        compiler_params=params(8),
+        cost_estimate=half_cost,
+        name="store_last",
+    )(n, n_ends, stored)
     new = pl.pallas_call(
         final_kernel,
         out_shape=shape(3, X, Y, Z),
-        in_specs=[VM] * 5,
+        in_specs=[VM] * 8,
         out_specs=ANY,
-        scratch_shapes=[pltpu.VMEM((3, X, Y, Z), F32)] + sems,
+        scratch_shapes=[pltpu.VMEM((3, X, Y, Z), F32), pltpu.SemaphoreType.DMA((GROUPS + 2,))],
         compiler_params=params(16),
         name="final",
-    )(w, r, joined, joined_other, other)
-    return new, n
+    )(w, r, w_ends, r_ends, start, joined, joined_other, other)
+    return new, stored
 
 
 def solution(mesh):

time: 39.7 us -> 38 us (0.957)
  waiting for transfers between devices: 3.88 us -> 0.73 us
  Pallas kernels: 10.5 us -> 12.2 us
  blocking collectives: 11.6 us -> 11.1 us
    ppermute x1, waiting for transfers between devices: 2.05 us -> 0.01 us  [shards(): rxb = lax.ppermute(xb, 'gx', pair_high(nx))]
    pallas_call x1 -> x4, Pallas kernels: 2.85 us -> 4.49 us  [the longest x1 1.83 us: shards(): pl.pallas_call(stencil_kernel, out_shape=[part_shape] * 3 + [shape(2, 3,...]
    ppermute x1, waiting for transfers between devices: 0.94 us -> 0.01 us  [shards(): other = lax.ppermute(mom, 'gx', pair_low(nx))]
    ppermute x1, waiting for transfers between devices: 0.88 us -> 0.01 us  [shards(): joined_other = lax.ppermute(joined, 'gx', pair_low(nx))]
    ppermute x1, waiting for transfers between devices: 0.01 us -> 0.72 us  [shards(): rza = lax.ppermute(za, 'gz', pair_low(nz))]
    all_to_all x1, blocking collectives: 11.6 us -> 11.1 us  [shards(): everyone = lax.all_to_all(chip, 'gx', 0, 0, axis_index_groups=groups)]
    ppermute x1, starting transfers between devices: 2.15 us -> 2.55 us  [shards(): other = lax.ppermute(mom, 'gx', pair_low(nx))]
  transfers between devices with their start and end apart: 6 -> 6, of which waited for: 3 -> 1; matrix products, arithmetic and copies ran while one was open for 0% -> 0% of each run, Pallas kernels for 0% -> 11%
where the time goes in v3:
time: 38 us; the launch traced here: 37.8 us
  starting transfers between devices  13.1 us (34%)
  Pallas kernels  12.2 us (32%)
  blocking collectives  11.1 us (29%)
  waiting for transfers between devices  0.73 us (2%)
  between operations  0.72 us (2%)
    all_to_all x1, blocking collectives, shards(): everyone = lax.all_to_all(chip, 'gx', 0, 0, axis_index_groups=groups)  11.1 us
    pallas_call x1, Pallas kernels, shards(): pl.pallas_call(pack_kernel, out_shape=[shape(208, Z), shape(200, Z)] + [s...  5.77 us
    ppermute x1, starting transfers between devices, shards(): rzb = lax.ppermute(zb, 'gz', pair_high(nz))  5.68 us
    ppermute x1, starting transfers between devices, shards(): other = lax.ppermute(mom, 'gx', pair_low(nx))  2.55 us
    pallas_call x1, Pallas kernels, shards(): pl.pallas_call(stencil_kernel, out_shape=[part_shape] * 3 + [shape(2, 3,...  1.83 us
    pallas_call x1, Pallas kernels, shards(): pl.pallas_call(final_kernel, out_shape=shape(3, X, Y, Z), in_specs=[VM] *...  1.82 us
    ppermute x1, starting transfers between devices, shards(): rxa = lax.ppermute(xa, 'gx', pair_low(nx))  1.75 us
    ppermute x1, starting transfers between devices, shards(): joined_other = lax.ppermute(joined, 'gx', pair_low(nx))  1.7 us
  transfers between devices with their start and end apart: 6, of which 1 were waited for; matrix products, arithmetic and copies ran while one was open for 0% of the time, Pallas kernels for 11%

profile of v3, /device:TPU:1, one launch (start us, length us, event | category | flops | bytes accessed | tf_op | source)
XLA Modules:
  0.0 37.8 jit_solution(14506368897116670419)
XLA Ops:
  0.6 5.8 %pack.1 = (f32[208,128]{1,0:T(8,128)S(1)}, f32[200,128]{1,0:T(8,128)S(1)}, f32[3,2,32,128]{3,2,1,0:T(8,128)S(1)}, f32[3,2,32,128]{3,2,1,0:T(8,128)S(1)}, f32[3,6...) custom-call(f32[3,64,32,128]{3,2,1,0:T(8,128)} %v_ref.1), custom_call_target="tpu_custom_call" | custom-call | tf_op jit(solution)/shard_map/pack/pallas_call | solution.py:355
  6.4 5.7 %collective-permute-start = (f32[208,128]{1,0:T(8,128)S(1)}, f32[208,128]{1,0:T(8,128)S(1)}, u32[]{:S(2)}, u32[]{:S(2)}) collective-permute-start(f32[208,128]{1,0:T(8,128)S(1)} %get-tuple-element.25.zb_ref), channel_id=1, source_target_pairs={{0,15},{1,2},{2,1},{3,4},{4,3},{5,6},{6,5},{7,8},{8,7},{9,10},{10,... | collective-permute-start | bytes 319496 | tf_op jit(solution)/shard_map/ppermute | solution.py:364
  12.1 0.1 collective-permute-start.1
  12.2 1.3 %collective-permute-start.2 = (f32[3,2,32,128]{3,2,1,0:T(8,128)S(1)}, f32[3,2,32,128]{3,2,1,0:T(8,128)S(1)}, u32[]{:S(2)}, u32[]{:S(2)}) collective-permute-start(f32[3,2,32,128]{3,2,1,0:T(8,128)S(1)} %get-tuple-element.30), channel_id=1, source_target_pairs={{0,240},{16,32},{32,16},{48,64},{64,48},{80,96},{96,80},{112,128},... | collective-permute-start | bytes 294920 | tf_op jit(solution)/shard_map/ppermute | solution.py:376
  13.5 1.7 %collective-permute-start.3 = (f32[3,2,32,128]{3,2,1,0:T(8,128)S(1)}, f32[3,2,32,128]{3,2,1,0:T(8,128)S(1)}, u32[]{:S(2)}, u32[]{:S(2)}) collective-permute-start(f32[3,2,32,128]{3,2,1,0:T(8,128)S(1)} %get-tuple-element.31), channel_id=1, source_target_pairs={{0,16},{16,0},{32,48},{48,32},{64,80},{80,64},{96,112},{112,96},{1... | collective-permute-start | bytes 294920 | tf_op jit(solution)/shard_map/ppermute | solution.py:377
  15.3 0.7 %collective-permute-done.1.ra_ref = f32[200,128]{1,0:T(8,128)S(1)} collective-permute-done((f32[200,128]{1,0:T(8,128)S(1)}, f32[200,128]{1,0:T(8,128)S(1)}, u32[]{:S(2)}, u32[]{:S(2)}) %collective-permute-start.1) | collective-permute-done | bytes 102432 | tf_op jit(solution)/shard_map/ppermute | solution.py:375
  16.0 0.0 collective-permute-done.rb_ref
  16.0 1.8 %stencil.1 = (f32[3,64,32,128]{3,2,1,0:T(8,128)S(1)}, f32[3,64,32,128]{3,2,1,0:T(8,128)S(1)}, f32[3,64,32,128]{3,2,1,0:T(8,128)S(1)}, f32[2,3,32,128]{3,2,1,0:T(8,128)S(1)}, f32[2,96,128]{2,1,0:T(8,128)S(1)}) custom-call(f32[3,64,48,128]{3,2,1,0:T(8,128)S(1)} %get-tuple-element.20.vp_ref, f32[3,64,32,128]{3,2,1,0:T(8,128)S(1)} %third.1.part_ref, ...), custom_call_target="tpu_custom_call" | custom-call | flops 20000000 | bytes 12000000 | tf_op jit(solution)/shard_map/stencil/pallas_call | solution.py:388
  17.8 0.0 collective-permute-done.2.xb_ref
  17.8 0.0 collective-permute-done.3.xa_ref
  17.9 0.4 ends.1
  18.2 2.6 %collective-permute-start.4 = (f32[2,3,32,128]{3,2,1,0:T(8,128)S(1)}, f32[2,3,32,128]{3,2,1,0:T(8,128)S(1)}, u32[]{:S(2)}, u32[]{:S(2)}) collective-permute-start(f32[2,3,32,128]{3,2,1,0:T(8,128)S(1)} %get-tuple-element.35.own_ref), channel_id=1, source_target_pairs={{0,16},{16,0},{32,48},{48,32},{64,80},{80,64},{96,112},{112,96},{1... | collective-permute-start | bytes 294920 | tf_op jit(solution)/shard_map/ppermute | solution.py:405
  20.8 1.1 %store_first.1.started_ref = f32[3,64,32,128]{3,2,1,0:T(8,128)} custom-call(f32[3,64,32,128]{3,2,1,0:T(8,128)S(1)} %get-tuple-element.36.n_ref, f32[3,4,32,128]{3,2,1,0:T(8,128)S(1)} %get-tuple-element.37.ends_ref), custom_call_target="tpu_custom_call" | custom-call | bytes 4000000 | tf_op jit(solution)/shard_map/store_first/pallas_call | solution.py:407
  21.9 0.0 collective-permute-done.4.other_ref
  22.0 11.1 %all_to_all.5.all_ref = f32[8,2,3,16,128]{4,3,2,1,0:T(8,128)S(1)} all-to-all(f32[8,2,3,16,128]{4,3,2,1,0:T(8,128)S(1)} %chip.1), channel_id=1, replica_groups={{0,32,64,96,128,160,192,224},{16,48,80,112,144,176,208,240},{1,33,65,97..., dimensions={0} | all-to-all | bytes 786432 | tf_op jit(solution)/shard_map/all_to_all | solution.py:428
  33.2 1.7 %collective-permute-start.5 = (f32[2,3,16,128]{3,2,1,0:T(8,128)S(1)}, f32[2,3,16,128]{3,2,1,0:T(8,128)S(1)}, u32[]{:S(2)}, u32[]{:S(2)}) collective-permute-start(f32[2,3,16,128]{3,2,1,0:T(8,128)S(1)} %join.1.in_own_ref), channel_id=1, source_target_pairs={{0,16},{16,0},{32,48},{48,32},{64,80},{80,64},{96,112},{112,96},{1... | collective-permute-start | bytes 147464 | tf_op jit(solution)/shard_map/ppermute | solution.py:437
  34.9 1.1 %store_last.1 = f32[3,64,32,128]{3,2,1,0:T(8,128)} custom-call(f32[3,64,32,128]{3,2,1,0:T(8,128)S(1)} %get-tuple-element.36.n_ref, f32[3,4,32,128]{3,2,1,0:T(8,128)S(1)} %get-tuple-element.37.ends_ref, f32[3,64,32,128]{3,2,1,0:T(8,128)} %store_first.1.started_ref), custom_call_target="tpu_custom_call", output_to_operand_aliasing={{}: (2, {})} | custom-call | bytes 4000000 | tf_op jit(solution)/shard_map/store_last/pallas_call | solution.py:438
  36.0 0.0 collective-permute-done.5.in_other_ref
  36.0 1.8 %final.1 = f32[3,64,32,128]{3,2,1,0:T(8,128)} custom-call(f32[3,64,32,128]{3,2,1,0:T(8,128)S(1)} %get-tuple-element.26.w_ref, f32[3,64,32,128]{3,2,1,0:T(8,128)S(1)} %get-tuple-element.27.r_ref, f32[3,4,32,128]{3,2,1,0:T(8,128)S(1)} %get-tuple-element.32.wend_ref, f32[3,4,32,128]{3,2,1,0:T(8,128)S(1)} %get-tuple-element.33.rend_ref, ...), custom_call_target="tpu_custom_call" | custom-call | tf_op jit(solution)/shard_map/final/pallas_call | solution.py:449
  (4 shorter events, 0.1 us)
Async XLA Ops:
  6.4 9.6 %collective-permute-start = (f32[208,128]{1,0:T(8,128)S(1)}, f32[208,128]{1,0:T(8,128)S(1)}, u32[]{:S(2)}, u32[]{:S(2)}) collective-permute-start(f32[208,128]{1,0:T(8,128)S(1)} %get-tuple-element.25.zb_ref), channel_id=1, source_target_pairs={{0,15},{1,2},{2,1},{3,4},{4,3},{5,6},{6,5},{7,8},{8,7},{9,10},{10,... | collective-permute-start | bytes 319496 | tf_op jit(solution)/shard_map/ppermute | solution.py:364
  12.1 3.9 %collective-permute-start.1 = (f32[200,128]{1,0:T(8,128)S(1)}, f32[200,128]{1,0:T(8,128)S(1)}, u32[]{:S(2)}, u32[]{:S(2)}) collective-permute-start(f32[200,128]{1,0:T(8,128)S(1)} %get-tuple-element.24.za_ref), channel_id=1, source_target_pairs={{0,1},{1,0},{2,3},{3,2},{4,5},{5,4},{6,7},{7,6},{8,9},{9,8},{10,11... | collective-permute-start | bytes 307208 | tf_op jit(solution)/shard_map/ppermute | solution.py:375
  12.2 5.6 %collective-permute-start.2 = (f32[3,2,32,128]{3,2,1,0:T(8,128)S(1)}, f32[3,2,32,128]{3,2,1,0:T(8,128)S(1)}, u32[]{:S(2)}, u32[]{:S(2)}) collective-permute-start(f32[3,2,32,128]{3,2,1,0:T(8,128)S(1)} %get-tuple-element.30), channel_id=1, source_target_pairs={{0,240},{16,32},{32,16},{48,64},{64,48},{80,96},{96,80},{112,128},... | collective-permute-start | bytes 294920 | tf_op jit(solution)/shard_map/ppermute | solution.py:376
  13.5 4.3 %collective-permute-start.3 = (f32[3,2,32,128]{3,2,1,0:T(8,128)S(1)}, f32[3,2,32,128]{3,2,1,0:T(8,128)S(1)}, u32[]{:S(2)}, u32[]{:S(2)}) collective-permute-start(f32[3,2,32,128]{3,2,1,0:T(8,128)S(1)} %get-tuple-element.31), channel_id=1, source_target_pairs={{0,16},{16,0},{32,48},{48,32},{64,80},{80,64},{96,112},{112,96},{1... | collective-permute-start | bytes 294920 | tf_op jit(solution)/shard_map/ppermute | solution.py:377
  18.2 3.7 %collective-permute-start.4 = (f32[2,3,32,128]{3,2,1,0:T(8,128)S(1)}, f32[2,3,32,128]{3,2,1,0:T(8,128)S(1)}, u32[]{:S(2)}, u32[]{:S(2)}) collective-permute-start(f32[2,3,32,128]{3,2,1,0:T(8,128)S(1)} %get-tuple-element.35.own_ref), channel_id=1, source_target_pairs={{0,16},{16,0},{32,48},{48,32},{64,80},{80,64},{96,112},{112,96},{1... | collective-permute-start | bytes 294920 | tf_op jit(solution)/shard_map/ppermute | solution.py:405
  33.2 2.9 %collective-permute-start.5 = (f32[2,3,16,128]{3,2,1,0:T(8,128)S(1)}, f32[2,3,16,128]{3,2,1,0:T(8,128)S(1)}, u32[]{:S(2)}, u32[]{:S(2)}) collective-permute-start(f32[2,3,16,128]{3,2,1,0:T(8,128)S(1)} %join.1.in_own_ref), channel_id=1, source_target_pairs={{0,16},{16,0},{32,48},{48,32},{64,80},{80,64},{96,112},{112,96},{1... | collective-permute-start | bytes 147464 | tf_op jit(solution)/shard_map/ppermute | solution.py:437

commit v4 on v3

--- a/solution.py
+++ b/solution.py
@@ -23,6 +23,8 @@
 LOAD = 16
 LOADS = X // LOAD
 GROUPS = (X - 4) // GROUP
+FIRST = 2 + 2 * GROUP
+SECOND = 2 + 4 * GROUP
 PAD = 8
 WIDE = Y + 2 * PAD
 CHIPS = 8
@@ -173,7 +175,7 @@
 
 def stencil_kernel(
     vp_ref, part_ref, za_ref, zb_ref, rb_ref, ra_ref,
-    n_ref, w_ref, r_ref, sum_ref, edge_ref,
+    n_ref, w_ref, r_ref, sum_ref, edge_ref, stored_ref, sem,
 ):
     z_even = lax.rem(lax.axis_index("gz"), 2) == 0
     lane = lanes(3 * Y)
@@ -204,10 +206,17 @@
             w_ref[:, x] = w
             r_ref[:, x] = p - f
             power = power * LAM
+
+        @pl.when(g == 1)
+        def _():
+            store.start()
+
         return p, q, power
 
+    store = pltpu.make_async_copy(n_ref.at[:, 2:FIRST], stored_ref.at[:, 2:FIRST], sem)
     zero = jnp.zeros((3, Y, Z), F32)
     sum_ref[0], sum_ref[1], _ = lax.fori_loop(0, GROUPS, group, (zero, zero, F32(1.0)))
+    store.wait()
 
 
 def ends_kernel(
@@ -246,9 +255,9 @@
     mom_ref[1] = sources[0] + LAM * sources[1] + LAM**2 * sum_ref[1] + ends
 
 
-def store_first_kernel(n_ref, ends_ref, out_ref, sems):
+def store_first_kernel(n_ref, ends_ref, started_ref, out_ref, sems):
     copies = [
-        pltpu.make_async_copy(n_ref.at[:, 2 : X // 2], out_ref.at[:, 2 : X // 2], sems.at[0]),
+        pltpu.make_async_copy(n_ref.at[:, FIRST:SECOND], out_ref.at[:, FIRST:SECOND], sems.at[0]),
         pltpu.make_async_copy(ends_ref.at[:, 0:2], out_ref.at[:, 0:2], sems.at[1]),
     ]
     for copy in copies:
@@ -259,7 +268,7 @@
 
 def store_last_kernel(n_ref, ends_ref, started_ref, out_ref, sems):
     copies = [
-        pltpu.make_async_copy(n_ref.at[:, X // 2 : X - 2], out_ref.at[:, X // 2 : X - 2], sems.at[0]),
+        pltpu.make_async_copy(n_ref.at[:, SECOND : X - 2], out_ref.at[:, SECOND : X - 2], sems.at[0]),
         pltpu.make_async_copy(ends_ref.at[:, 2:4], out_ref.at[:, X - 2 : X], sems.at[1]),
     ]
     for copy in copies:
@@ -385,11 +394,12 @@
         cost_estimate=COST,
         name="third",
     )(vp, part)
-    n, w, r, sums, edge = pl.pallas_call(
+    n, w, r, sums, edge, stored = pl.pallas_call(
         stencil_kernel,
-        out_shape=[part_shape] * 3 + [shape(2, 3, Y, Z), shape(2, 3 * Y, Z)],
+        out_shape=[part_shape] * 3 + [shape(2, 3, Y, Z), shape(2, 3 * Y, Z), shape(3, X, Y, Z)],
         in_specs=[VM] * 6,
-        out_specs=[VM] * 5,
+        out_specs=[VM] * 5 + [HBM],
+        scratch_shapes=[pltpu.SemaphoreType.DMA(())],
         compiler_params=params(16),
         cost_estimate=COST,
         name="stencil",
@@ -407,13 +417,14 @@
     stored = pl.pallas_call(
         store_first_kernel,
         out_shape=shape(3, X, Y, Z),
-        in_specs=[VM] * 2,
+        in_specs=[VM, VM, HBM],
         out_specs=HBM,
+        input_output_aliases={2: 0},
         scratch_shapes=[pltpu.SemaphoreType.DMA((2,))],
         compiler_params=params(8),
         cost_estimate=half_cost,
         name="store_first",
-    )(n, n_ends)
+    )(n, n_ends, stored)
     stored = pltpu.with_memory_space_constraint(stored, pltpu.HBM)
     half = (2, 3, Y // 2, Z)
     chip = pl.pallas_call(

time: 38 us -> 37.7 us (level)
  transfers between devices with their start and end apart: 6 -> 6, of which waited for: 1 -> 1; matrix products, arithmetic and copies ran while one was open for 0% -> 0% of each run, Pallas kernels for 11% -> 10%
where the time goes in v4:
time: 37.7 us; the launch traced here: 37.5 us
  starting transfers between devices  13.3 us (35%)
  Pallas kernels  11.9 us (32%)
  blocking collectives  11 us (29%)
  waiting for transfers between devices  0.73 us (2%)
  between operations  0.72 us (2%)
    all_to_all x1, blocking collectives, shards(): everyone = lax.all_to_all(chip, 'gx', 0, 0, axis_index_groups=groups)  11 us
    pallas_call x1, Pallas kernels, shards(): pl.pallas_call(pack_kernel, out_shape=[shape(208, Z), shape(200, Z)] + [s...  5.77 us
    ppermute x1, starting transfers between devices, shards(): rzb = lax.ppermute(zb, 'gz', pair_high(nz))  5.68 us
    ppermute x1, starting transfers between devices, shards(): other = lax.ppermute(mom, 'gx', pair_low(nx))  2.56 us
    ppermute x1, starting transfers between devices, shards(): joined_other = lax.ppermute(joined, 'gx', pair_low(nx))  1.86 us
    pallas_call x1, Pallas kernels, shards(): pl.pallas_call(stencil_kernel, out_shape=[part_shape] * 3 + [shape(2, 3,...  1.86 us
    pallas_call x1, Pallas kernels, shards(): pl.pallas_call(final_kernel, out_shape=shape(3, X, Y, Z), in_specs=[VM] *...  1.82 us
    ppermute x1, starting transfers between devices, shards(): rxa = lax.ppermute(xa, 'gx', pair_low(nx))  1.75 us
  transfers between devices with their start and end apart: 6, of which 1 were waited for; matrix products, arithmetic and copies ran while one was open for 0% of the time, Pallas kernels for 10%

profile of v4, /device:TPU:1, one launch (start us, length us, event | category | flops | bytes accessed | tf_op | source)
XLA Modules:
  0.0 37.5 jit_solution(7808855500770338667)
XLA Ops:
  0.6 5.8 %pack.1 = (f32[208,128]{1,0:T(8,128)S(1)}, f32[200,128]{1,0:T(8,128)S(1)}, f32[3,2,32,128]{3,2,1,0:T(8,128)S(1)}, f32[3,2,32,128]{3,2,1,0:T(8,128)S(1)}, f32[3,6...) custom-call(f32[3,64,32,128]{3,2,1,0:T(8,128)} %v_ref.1), custom_call_target="tpu_custom_call" | custom-call | tf_op jit(solution)/shard_map/pack/pallas_call | solution.py:364
  6.4 5.7 %collective-permute-start = (f32[208,128]{1,0:T(8,128)S(1)}, f32[208,128]{1,0:T(8,128)S(1)}, u32[]{:S(2)}, u32[]{:S(2)}) collective-permute-start(f32[208,128]{1,0:T(8,128)S(1)} %get-tuple-element.26.zb_ref), channel_id=1, source_target_pairs={{0,15},{1,2},{2,1},{3,4},{4,3},{5,6},{6,5},{7,8},{8,7},{9,10},{10,... | collective-permute-start | bytes 319496 | tf_op jit(solution)/shard_map/ppermute | solution.py:373
  12.1 0.1 collective-permute-start.1
  12.2 1.3 %collective-permute-start.2 = (f32[3,2,32,128]{3,2,1,0:T(8,128)S(1)}, f32[3,2,32,128]{3,2,1,0:T(8,128)S(1)}, u32[]{:S(2)}, u32[]{:S(2)}) collective-permute-start(f32[3,2,32,128]{3,2,1,0:T(8,128)S(1)} %get-tuple-element.31), channel_id=1, source_target_pairs={{0,240},{16,32},{32,16},{48,64},{64,48},{80,96},{96,80},{112,128},... | collective-permute-start | bytes 294920 | tf_op jit(solution)/shard_map/ppermute | solution.py:385
  13.5 1.7 %collective-permute-start.3 = (f32[3,2,32,128]{3,2,1,0:T(8,128)S(1)}, f32[3,2,32,128]{3,2,1,0:T(8,128)S(1)}, u32[]{:S(2)}, u32[]{:S(2)}) collective-permute-start(f32[3,2,32,128]{3,2,1,0:T(8,128)S(1)} %get-tuple-element.32), channel_id=1, source_target_pairs={{0,16},{16,0},{32,48},{48,32},{64,80},{80,64},{96,112},{112,96},{1... | collective-permute-start | bytes 294920 | tf_op jit(solution)/shard_map/ppermute | solution.py:386
  15.3 0.7 %collective-permute-done.1.ra_ref = f32[200,128]{1,0:T(8,128)S(1)} collective-permute-done((f32[200,128]{1,0:T(8,128)S(1)}, f32[200,128]{1,0:T(8,128)S(1)}, u32[]{:S(2)}, u32[]{:S(2)}) %collective-permute-start.1) | collective-permute-done | bytes 102432 | tf_op jit(solution)/shard_map/ppermute | solution.py:384
  16.0 0.0 collective-permute-done.rb_ref
  16.0 1.9 %stencil.1 = (f32[3,64,32,128]{3,2,1,0:T(8,128)S(1)}, f32[3,64,32,128]{3,2,1,0:T(8,128)S(1)}, f32[3,64,32,128]{3,2,1,0:T(8,128)S(1)}, f32[2,3,32,128]{3,2,1,0:T(...) custom-call(f32[3,64,48,128]{3,2,1,0:T(8,128)S(1)} %get-tuple-element.21.vp_ref, ...), custom_call_target="tpu_custom_call" | custom-call | flops 20000000 | bytes 12000000 | tf_op jit(solution)/shard_map/stencil/pallas_call | solution.py:397
  17.9 0.0 collective-permute-done.2.xb_ref
  17.9 0.0 collective-permute-done.3.xa_ref
  17.9 0.4 ends.1
  18.3 2.6 %collective-permute-start.4 = (f32[2,3,32,128]{3,2,1,0:T(8,128)S(1)}, f32[2,3,32,128]{3,2,1,0:T(8,128)S(1)}, u32[]{:S(2)}, u32[]{:S(2)}) collective-permute-start(f32[2,3,32,128]{3,2,1,0:T(8,128)S(1)} %get-tuple-element.36.own_ref), channel_id=1, source_target_pairs={{0,16},{16,0},{32,48},{48,32},{64,80},{80,64},{96,112},{112,96},{1... | collective-permute-start | bytes 294920 | tf_op jit(solution)/shard_map/ppermute | solution.py:415
  20.8 1.0 %store_first.1.started_ref = f32[3,64,32,128]{3,2,1,0:T(8,128)} custom-call(f32[3,64,32,128]{3,2,1,0:T(8,128)S(1)} %get-tuple-element.37.n_ref, f32[3,4,32,128]{3,2,1,0:T(8,128)S(1)} %get-tuple-element.38.ends_ref, f32[3,64,32,128]{3,2,1,0:T(8,128)} %get-tuple-element.39.started_ref), custom_call_target="tpu_custom_call", output_to_operand_aliasing={{}: (2, {})} | custom-call | bytes 4000000 | tf_op jit(solution)/shard_map/store_first/pallas_call | solution.py:417
  21.8 0.0 collective-permute-done.4.other_ref
  21.9 11.0 %all_to_all.5.all_ref = f32[8,2,3,16,128]{4,3,2,1,0:T(8,128)S(1)} all-to-all(f32[8,2,3,16,128]{4,3,2,1,0:T(8,128)S(1)} %chip.1), channel_id=1, replica_groups={{0,32,64,96,128,160,192,224},{16,48,80,112,144,176,208,240},{1,33,65,97..., dimensions={0} | all-to-all | bytes 786432 | tf_op jit(solution)/shard_map/all_to_all | solution.py:439
  32.9 1.9 %collective-permute-start.5 = (f32[2,3,16,128]{3,2,1,0:T(8,128)S(1)}, f32[2,3,16,128]{3,2,1,0:T(8,128)S(1)}, u32[]{:S(2)}, u32[]{:S(2)}) collective-permute-start(f32[2,3,16,128]{3,2,1,0:T(8,128)S(1)} %join.1.in_own_ref), channel_id=1, source_target_pairs={{0,16},{16,0},{32,48},{48,32},{64,80},{80,64},{96,112},{112,96},{1... | collective-permute-start | bytes 147464 | tf_op jit(solution)/shard_map/ppermute | solution.py:448
  34.7 1.0 %store_last.1 = f32[3,64,32,128]{3,2,1,0:T(8,128)} custom-call(f32[3,64,32,128]{3,2,1,0:T(8,128)S(1)} %get-tuple-element.37.n_ref, f32[3,4,32,128]{3,2,1,0:T(8,128)S(1)} %get-tuple-element.38.ends_ref, f32[3,64,32,128]{3,2,1,0:T(8,128)} %store_first.1.started_ref), custom_call_target="tpu_custom_call", output_to_operand_aliasing={{}: (2, {})} | custom-call | bytes 4000000 | tf_op jit(solution)/shard_map/store_last/pallas_call | solution.py:449
  35.7 0.0 collective-permute-done.5.in_other_ref
  35.7 1.8 %final.1 = f32[3,64,32,128]{3,2,1,0:T(8,128)} custom-call(f32[3,64,32,128]{3,2,1,0:T(8,128)S(1)} %get-tuple-element.27.w_ref, f32[3,64,32,128]{3,2,1,0:T(8,128)S(1)} %get-tuple-element.28.r_ref, f32[3,4,32,128]{3,2,1,0:T(8,128)S(1)} %get-tuple-element.33.wend_ref, f32[3,4,32,128]{3,2,1,0:T(8,128)S(1)} %get-tuple-element.34.rend_ref, ...), custom_call_target="tpu_custom_call" | custom-call | tf_op jit(solution)/shard_map/final/pallas_call | solution.py:460
  (4 shorter events, 0.1 us)
Async XLA Ops:
  6.4 9.6 %collective-permute-start = (f32[208,128]{1,0:T(8,128)S(1)}, f32[208,128]{1,0:T(8,128)S(1)}, u32[]{:S(2)}, u32[]{:S(2)}) collective-permute-start(f32[208,128]{1,0:T(8,128)S(1)} %get-tuple-element.26.zb_ref), channel_id=1, source_target_pairs={{0,15},{1,2},{2,1},{3,4},{4,3},{5,6},{6,5},{7,8},{8,7},{9,10},{10,... | collective-permute-start | bytes 319496 | tf_op jit(solution)/shard_map/ppermute | solution.py:373
  12.1 3.9 %collective-permute-start.1 = (f32[200,128]{1,0:T(8,128)S(1)}, f32[200,128]{1,0:T(8,128)S(1)}, u32[]{:S(2)}, u32[]{:S(2)}) collective-permute-start(f32[200,128]{1,0:T(8,128)S(1)} %get-tuple-element.25.za_ref), channel_id=1, source_target_pairs={{0,1},{1,0},{2,3},{3,2},{4,5},{5,4},{6,7},{7,6},{8,9},{9,8},{10,11... | collective-permute-start | bytes 307208 | tf_op jit(solution)/shard_map/ppermute | solution.py:384
  12.2 5.7 %collective-permute-start.2 = (f32[3,2,32,128]{3,2,1,0:T(8,128)S(1)}, f32[3,2,32,128]{3,2,1,0:T(8,128)S(1)}, u32[]{:S(2)}, u32[]{:S(2)}) collective-permute-start(f32[3,2,32,128]{3,2,1,0:T(8,128)S(1)} %get-tuple-element.31), channel_id=1, source_target_pairs={{0,240},{16,32},{32,16},{48,64},{64,48},{80,96},{96,80},{112,128},... | collective-permute-start | bytes 294920 | tf_op jit(solution)/shard_map/ppermute | solution.py:385
  13.5 4.3 %collective-permute-start.3 = (f32[3,2,32,128]{3,2,1,0:T(8,128)S(1)}, f32[3,2,32,128]{3,2,1,0:T(8,128)S(1)}, u32[]{:S(2)}, u32[]{:S(2)}) collective-permute-start(f32[3,2,32,128]{3,2,1,0:T(8,128)S(1)} %get-tuple-element.32), channel_id=1, source_target_pairs={{0,16},{16,0},{32,48},{48,32},{64,80},{80,64},{96,112},{112,96},{1... | collective-permute-start | bytes 294920 | tf_op jit(solution)/shard_map/ppermute | solution.py:386
  18.3 3.5 %collective-permute-start.4 = (f32[2,3,32,128]{3,2,1,0:T(8,128)S(1)}, f32[2,3,32,128]{3,2,1,0:T(8,128)S(1)}, u32[]{:S(2)}, u32[]{:S(2)}) collective-permute-start(f32[2,3,32,128]{3,2,1,0:T(8,128)S(1)} %get-tuple-element.36.own_ref), channel_id=1, source_target_pairs={{0,16},{16,0},{32,48},{48,32},{64,80},{80,64},{96,112},{112,96},{1... | collective-permute-start | bytes 294920 | tf_op jit(solution)/shard_map/ppermute | solution.py:415
  32.9 2.8 %collective-permute-start.5 = (f32[2,3,16,128]{3,2,1,0:T(8,128)S(1)}, f32[2,3,16,128]{3,2,1,0:T(8,128)S(1)}, u32[]{:S(2)}, u32[]{:S(2)}) collective-permute-start(f32[2,3,16,128]{3,2,1,0:T(8,128)S(1)} %join.1.in_own_ref), channel_id=1, source_target_pairs={{0,16},{16,0},{32,48},{48,32},{64,80},{80,64},{96,112},{112,96},{1... | collective-permute-start | bytes 147464 | tf_op jit(solution)/shard_map/ppermute | solution.py:448
